TPU v7x, 32 devices: a whole 2x2x4 slice. The times are simulated.
32 devices in a mesh: fsdp: 2 (over x), ctx: 16 (over z, y, core).
Axes of the slice: x: 2, y: 2, z: 4, core: 2. Of those that a mesh axis runs over, the one named last changes fastest.
Arguments:
- tokens: bfloat16 [1024, 4, 768], P('ctx', 'fsdp'), may hold values from -6 to 6
- lengths: int32 [4], P('fsdp'), may hold values from 1 to 1024, as said below
- cotangent: bfloat16 [1024, 4, 768], P('ctx', 'fsdp'), may hold values from -6 to 6
- attend_weight: float32 [3, 768, 768], P(None, 'fsdp', 'ctx'), may hold values from -0.3125 to 0.3125
- attend_first: float32 [3, 768, 768], P(None, 'fsdp', 'ctx'), may hold values from -32 to 32
- attend_second: float32 [3, 768, 768], P(None, 'fsdp', 'ctx'), may hold values from 2.048 to 8.192
- output_weight: float32 [768, 768], P('fsdp', 'ctx'), may hold values from -0.875 to 0.875
- output_first: float32 [768, 768], P('fsdp', 'ctx'), may hold values from -6 to 6
- output_second: float32 [768, 768], P('fsdp', 'ctx'), may hold values from 0.04096 to 0.16384
- expand_weight: float32 [768, 3072], P('fsdp', 'ctx'), may hold values from -0.21875 to 0.21875
- expand_first: float32 [768, 3072], P('fsdp', 'ctx'), may hold values from -6 to 6
- expand_second: float32 [768, 3072], P('fsdp', 'ctx'), may hold values from 0.16384 to 0.65536
- contract_weight: float32 [3072, 768], P('fsdp', 'ctx'), may hold values from -0.109375 to 0.109375
- contract_first: float32 [3072, 768], P('fsdp', 'ctx'), may hold values from -16 to 16
- contract_second: float32 [3072, 768], P('fsdp', 'ctx'), may hold values from 0.65536 to 2.62144
- vector_params: float32 [9216], P('ctx'), may hold values from -0.6 to 1.45
- vector_first: float32 [9216], P('ctx'), may hold values from -32 to 32
- vector_second: float32 [9216], P('ctx'), may hold values from 2.048 to 8.192
Outputs:
- layer_out: bfloat16 [1024, 4, 768], P('ctx', 'fsdp')
- tokens_grad: float32 [1024, 4, 768], P('ctx', 'fsdp')
- new_attend: float32 [3, 768, 768], P(None, 'fsdp', 'ctx')
- new_attend_first: float32 [3, 768, 768], P(None, 'fsdp', 'ctx')
- new_attend_second: float32 [3, 768, 768], P(None, 'fsdp', 'ctx')
- new_output: float32 [768, 768], P('fsdp', 'ctx')
- new_output_first: float32 [768, 768], P('fsdp', 'ctx')
- new_output_second: float32 [768, 768], P('fsdp', 'ctx')
- new_expand: float32 [768, 3072], P('fsdp', 'ctx')
- new_expand_first: float32 [768, 3072], P('fsdp', 'ctx')
- new_expand_second: float32 [768, 3072], P('fsdp', 'ctx')
- new_contract: float32 [3072, 768], P('fsdp', 'ctx')
- new_contract_first: float32 [3072, 768], P('fsdp', 'ctx')
- new_contract_second: float32 [3072, 768], P('fsdp', 'ctx')
- new_vector: float32 [9216], P('ctx')
- new_vector_first: float32 [9216], P('ctx')
- new_vector_second: float32 [9216], P('ctx')
Inputs may be any that keep to these rules, and one draw needn't show every extreme that they name: `lengths`: in each group of 2 consecutive sequences one, drawn from the seed, has all 1024 positions valid.
All inputs are finite; a program needn't handle non-finite values.
Results may differ from a plain program's by a relative error of at most 0.013.
The roundings to bfloat16 on the way count: a program that leaves them out, or rounds other values in their place, can miss the bound.
Values may be sent and summed in bfloat16 or wider, within the bound.
A program may use at most 192 MiB of HBM per device.

v0:
```python
import math

import jax
import jax.numpy as jnp
from jax import lax
from jax.sharding import PartitionSpec as P

D = 768
HEADS = 12
HEAD_DIM = 64
FF = 3072
STEP = 10


NORM_EPSILON = 1e-06
MASK_FILL = -1e30
BETA_ONE = 0.9
BETA_TWO = 0.999
ADAM_EPSILON = 1e-08
WEIGHT_DECAY = 0.01
RATE_ATTEND = 0.08
RATE_OUTPUT = 0.2
RATE_EXPAND = 0.05
RATE_CONTRACT = 0.025
RATE_VECTOR = 0.3


def norm_parts(values, gain, shift):
    centre = values - jnp.mean(values, axis=-1, keepdims=True)
    spread = jnp.mean(centre * centre, axis=-1, keepdims=True)
    inverse = lax.rsqrt(spread + NORM_EPSILON)
    normed = centre * inverse
    return (normed * gain + shift, normed, inverse)


def norm_back(grad_out, normed, inverse, gain):
    scaled = grad_out * gain
    centred = scaled - jnp.mean(scaled, axis=-1, keepdims=True)
    return inverse * (centred - normed * jnp.mean(scaled * normed, axis=-1, keepdims=True))


def exact_gelu(values):
    return jax.nn.gelu(values, approximate=False)


def adam_step(weight, first, second, grad, rate, decay):
    new_first = BETA_ONE * first + (1.0 - BETA_ONE) * grad
    new_second = BETA_TWO * second + (1.0 - BETA_TWO) * grad * grad
    first_hat = new_first / (1.0 - BETA_ONE**STEP)
    second_hat = new_second / (1.0 - BETA_TWO**STEP)
    new_weight = weight - rate * (
        first_hat / (jnp.sqrt(second_hat) + ADAM_EPSILON) + decay * weight
    )
    return (new_weight, new_first, new_second)


def on_device(
    tokens,
    lengths,
    cotangent,
    attend_weight,
    attend_first,
    attend_second,
    output_weight,
    output_first,
    output_second,
    expand_weight,
    expand_first,
    expand_second,
    contract_weight,
    contract_first,
    contract_second,
    vector_params,
    vector_first,
    vector_second,
):
    block, count, width = tokens.shape
    token_rows = block * count
    row_tiles = (
        lax.all_gather(attend_weight.astype(jnp.bfloat16), "fsdp", axis=1, tiled=True),
        lax.all_gather(output_weight.astype(jnp.bfloat16), "fsdp", axis=0, tiled=True),
        lax.all_gather(expand_weight.astype(jnp.bfloat16), "fsdp", axis=0, tiled=True),
        lax.all_gather(contract_weight.astype(jnp.bfloat16), "fsdp", axis=0, tiled=True),
    )
    attend_full, output_full, expand_full, contract_full = (
        lax.all_gather(row_tiles[0], "ctx", axis=2, tiled=True),
        lax.all_gather(row_tiles[1], "ctx", axis=1, tiled=True),
        lax.all_gather(row_tiles[2], "ctx", axis=1, tiled=True),
        lax.all_gather(row_tiles[3], "ctx", axis=1, tiled=True),
    )
    vector = lax.all_gather(vector_params, "ctx", axis=0, tiled=True)
    bias_query = vector[0:D]
    bias_value = vector[D : 2 * D]
    bias_out = vector[2 * D : 3 * D]
    bias_contract = vector[3 * D : 4 * D]
    gain_one = vector[4 * D : 5 * D]
    shift_one = vector[5 * D : 6 * D]
    gain_two = vector[6 * D : 7 * D]
    shift_two = vector[7 * D : 8 * D]
    bias_expand = vector[8 * D : 8 * D + FF]
    rows_in = tokens.reshape(token_rows, width)
    proj = jnp.einsum("td,cde->cte", rows_in, attend_full, preferred_element_type=jnp.float32)
    query = (proj[0] + bias_query).astype(jnp.bfloat16)
    local_keys = proj[1].astype(jnp.bfloat16).reshape(block, count, width)
    local_values = (proj[2] + bias_value).astype(jnp.bfloat16).reshape(block, count, width)
    all_keys, all_values = (
        lax.all_gather(local_keys, "ctx", axis=0, tiled=True),
        lax.all_gather(local_values, "ctx", axis=0, tiled=True),
    )
    seq_len = all_keys.shape[0]
    valid = (jnp.arange(seq_len, dtype=jnp.int32)[None, :] < lengths[:, None])[:, None, None, :]
    scale = 1.0 / math.sqrt(HEAD_DIM)
    head_query = query.reshape(block, count, HEADS, HEAD_DIM)

    def masked_scores(key_rows):
        key_heads = key_rows.reshape(seq_len, count, HEADS, HEAD_DIM)
        scores = (
            jnp.einsum("qshd,kshd->shqk", head_query, key_heads, preferred_element_type=jnp.float32)
            * scale
        )
        return jnp.where(valid, scores, MASK_FILL)

    masked = masked_scores(all_keys)
    peak = jnp.max(masked, axis=-1, keepdims=True)
    log_total = peak + jnp.log(jnp.sum(jnp.exp(masked - peak), axis=-1, keepdims=True))
    probs_low = jnp.exp(masked - log_total).astype(jnp.bfloat16)
    value_heads = all_values.reshape(seq_len, count, HEADS, HEAD_DIM)
    context = jnp.einsum(
        "shqk,kshd->qshd", probs_low, value_heads, preferred_element_type=jnp.float32
    )
    context = context.reshape(token_rows, width).astype(jnp.bfloat16)
    attn = jnp.dot(context, output_full, preferred_element_type=jnp.float32) + bias_out
    mixed, normed_one, inverse_one = norm_parts(
        rows_in.astype(jnp.float32) + attn, gain_one, shift_one
    )
    mixed_low = mixed.astype(jnp.bfloat16)
    pre = jnp.dot(mixed_low, expand_full, preferred_element_type=jnp.float32) + bias_expand
    act, gelu_back = jax.vjp(exact_gelu, pre)
    act_low = act.astype(jnp.bfloat16)
    ffn = jnp.dot(act_low, contract_full, preferred_element_type=jnp.float32) + bias_contract
    layer_out, normed_two, inverse_two = norm_parts(mixed + ffn, gain_two, shift_two)
    grad_out = cotangent.reshape(token_rows, width).astype(jnp.float32)
    grad_gain_two = jnp.sum(grad_out * normed_two, axis=0)
    grad_shift_two = jnp.sum(grad_out, axis=0)
    grad_resid = norm_back(grad_out, normed_two, inverse_two, gain_two)
    grad_ffn = grad_resid.astype(jnp.bfloat16)
    grad_bias_contract = jnp.sum(grad_ffn, axis=0, dtype=jnp.float32)
    grad_contract = jnp.einsum("tf,td->fd", act_low, grad_ffn, preferred_element_type=jnp.float32)
    grad_act = jnp.einsum("td,fd->tf", grad_ffn, contract_full, preferred_element_type=jnp.float32)
    grad_pre = gelu_back(grad_act)[0].astype(jnp.bfloat16)
    grad_bias_expand = jnp.sum(grad_pre, axis=0, dtype=jnp.float32)
    grad_expand = jnp.einsum("td,tf->df", mixed_low, grad_pre, preferred_element_type=jnp.float32)
    grad_mixed = grad_resid + jnp.einsum(
        "tf,df->td", grad_pre, expand_full, preferred_element_type=jnp.float32
    )
    grad_gain_one = jnp.sum(grad_mixed * normed_one, axis=0)
    grad_shift_one = jnp.sum(grad_mixed, axis=0)
    grad_attn = norm_back(grad_mixed, normed_one, inverse_one, gain_one)
    grad_attn_low = grad_attn.astype(jnp.bfloat16)
    grad_bias_out = jnp.sum(grad_attn_low, axis=0, dtype=jnp.float32)
    grad_output = jnp.einsum(
        "te,td->ed", context, grad_attn_low, preferred_element_type=jnp.float32
    )
    grad_context = jnp.einsum(
        "td,ed->te", grad_attn_low, output_full, preferred_element_type=jnp.float32
    ).astype(jnp.bfloat16)
    key_rows, value_rows = (all_keys, all_values)
    probs_full = jnp.exp(masked_scores(key_rows) - log_total)
    key_heads = key_rows.reshape(seq_len, count, HEADS, HEAD_DIM)
    value_back = value_rows.reshape(seq_len, count, HEADS, HEAD_DIM)
    context_heads = grad_context.reshape(block, count, HEADS, HEAD_DIM)
    grad_probs = jnp.einsum(
        "qshd,kshd->shqk", context_heads, value_back, preferred_element_type=jnp.float32
    )
    inner = jnp.sum(probs_full * grad_probs, axis=-1, keepdims=True)
    grad_scores = (probs_full * (grad_probs - inner)).astype(jnp.bfloat16)
    grad_query = (
        jnp.einsum("shqk,kshd->qshd", grad_scores, key_heads, preferred_element_type=jnp.float32)
        * scale
    )
    grad_query = grad_query.reshape(token_rows, width).astype(jnp.bfloat16)
    probs_back = probs_full.astype(jnp.bfloat16)
    size = lax.axis_size("ctx") * block
    grad_keys = (
        jnp.einsum("shqk,qshd->kshd", grad_scores, head_query, preferred_element_type=jnp.float32)
        * scale
    )
    grad_values = jnp.einsum(
        "shqk,qshd->kshd", probs_back, context_heads, preferred_element_type=jnp.float32
    )
    summed = lax.psum_scatter(
        jnp.concatenate(
            [grad_keys.reshape(size, count, width), grad_values.reshape(size, count, width)], axis=2
        ),
        "ctx",
        scatter_dimension=0,
        tiled=True,
    )
    grad_keys_low = summed[:, :, :width].reshape(token_rows, width).astype(jnp.bfloat16)
    grad_values_low = summed[:, :, width:].reshape(token_rows, width).astype(jnp.bfloat16)
    stacked = jnp.stack([grad_query, grad_keys_low, grad_values_low])
    grad_attend = jnp.einsum("td,cte->cde", rows_in, stacked, preferred_element_type=jnp.float32)
    tokens_grad = grad_attn + jnp.einsum(
        "cte,cde->td", stacked, attend_full, preferred_element_type=jnp.float32
    )
    grad_vector = jnp.concatenate(
        [
            jnp.sum(grad_query, axis=0, dtype=jnp.float32),
            jnp.sum(grad_values_low, axis=0, dtype=jnp.float32),
            grad_bias_out,
            grad_bias_contract,
            grad_gain_one,
            grad_shift_one,
            grad_gain_two,
            grad_shift_two,
            grad_bias_expand,
        ]
    )
    vector_total = lax.psum(grad_vector, "fsdp")
    column_parts = (
        lax.psum_scatter(grad_attend, "ctx", scatter_dimension=2, tiled=True),
        lax.psum_scatter(grad_output, "ctx", scatter_dimension=1, tiled=True),
        lax.psum_scatter(grad_expand, "ctx", scatter_dimension=1, tiled=True),
        lax.psum_scatter(grad_contract, "ctx", scatter_dimension=1, tiled=True),
        lax.psum_scatter(vector_total, "ctx", scatter_dimension=0, tiled=True),
    )
    owned = (
        lax.psum_scatter(column_parts[0], "fsdp", scatter_dimension=1, tiled=True),
        lax.psum_scatter(column_parts[1], "fsdp", scatter_dimension=0, tiled=True),
        lax.psum_scatter(column_parts[2], "fsdp", scatter_dimension=0, tiled=True),
        lax.psum_scatter(column_parts[3], "fsdp", scatter_dimension=0, tiled=True),
    )
    vector_owned = column_parts[4]
    attend_new = adam_step(
        attend_weight, attend_first, attend_second, owned[0], RATE_ATTEND, WEIGHT_DECAY
    )
    output_new = adam_step(
        output_weight, output_first, output_second, owned[1], RATE_OUTPUT, WEIGHT_DECAY
    )
    expand_new = adam_step(
        expand_weight, expand_first, expand_second, owned[2], RATE_EXPAND, WEIGHT_DECAY
    )
    contract_new = adam_step(
        contract_weight, contract_first, contract_second, owned[3], RATE_CONTRACT, WEIGHT_DECAY
    )
    vector_new = adam_step(
        vector_params, vector_first, vector_second, vector_owned, RATE_VECTOR, 0.0
    )
    return (
        layer_out.reshape(block, count, width).astype(jnp.bfloat16),
        tokens_grad.reshape(block, count, width),
        attend_new[0],
        attend_new[1],
        attend_new[2],
        output_new[0],
        output_new[1],
        output_new[2],
        expand_new[0],
        expand_new[1],
        expand_new[2],
        contract_new[0],
        contract_new[1],
        contract_new[2],
        vector_new[0],
        vector_new[1],
        vector_new[2],
    )


def solution(mesh):
    in_specs = (
        P("ctx", "fsdp", None),
        P("fsdp"),
        P("ctx", "fsdp", None),
        P(None, "fsdp", "ctx"),
        P(None, "fsdp", "ctx"),
        P(None, "fsdp", "ctx"),
        P("fsdp", "ctx"),
        P("fsdp", "ctx"),
        P("fsdp", "ctx"),
        P("fsdp", "ctx"),
        P("fsdp", "ctx"),
        P("fsdp", "ctx"),
        P("fsdp", "ctx"),
        P("fsdp", "ctx"),
        P("fsdp", "ctx"),
        P("ctx"),
        P("ctx"),
        P("ctx"),
    )
    out_specs = (
        P("ctx", "fsdp", None),
        P("ctx", "fsdp", None),
        P(None, "fsdp", "ctx"),
        P(None, "fsdp", "ctx"),
        P(None, "fsdp", "ctx"),
        P("fsdp", "ctx"),
        P("fsdp", "ctx"),
        P("fsdp", "ctx"),
        P("fsdp", "ctx"),
        P("fsdp", "ctx"),
        P("fsdp", "ctx"),
        P("fsdp", "ctx"),
        P("fsdp", "ctx"),
        P("fsdp", "ctx"),
        P("ctx"),
        P("ctx"),
        P("ctx"),
    )
    return jax.shard_map(
        on_device, mesh=mesh, in_specs=in_specs, out_specs=out_specs, check_vma=False
    )
```

profile of v0, /device:TPU:0, one launch (start us, length us, event | category | flops | bytes accessed | tf_op | source)
XLA Modules:
  0.0 1093.2 jit_solution(13563977809617758803)
XLA Ops:
  8.2 6.8 all_gather.33
  16.1 1.3 fusion.46
  18.9 61.5 %all-reduce = f32[9216]{0:T(1024)S(1)} all-reduce(f32[9216]{0:T(1024)S(1)} %dynamic-update-slice), channel_id=1, replica_groups=mesh['fsdp'=2,'ctx'=16] {'ctx'}, use_global_device_ids=true, to_apply=%add | all-reduce | flops 9216 | bytes 73728
  81.0 3.3 convolution_bitcast_fusion.1
  86.4 4.7 all_gather.38
  91.3 5.9 all_gather.40
  97.3 5.9 all_gather.42
  108.2 19.9 %all-gather.9.cloned.1.call-done = bf16[1024,2,768]{2,1,0:T(2,128)(2,1)} async-done(((bf16[64,2,768]{2,1,0:T(2,128)(2,1)}), bf16[1024,2,768]{2,1,0:T(2,128)(2,1)}) %all-gather.9.cloned.1.call-update) | async-done | bytes 3145744 | tf_op jit(solution)/shard_map/all_gather | solution.py:108
  128.1 7.0 copy.55
  135.1 39.9 %all-gather.11.cloned.1.call-done = bf16[1024,2,768]{2,1,0:T(2,128)(2,1)} async-done(((bf16[64,2,768]{2,1,0:T(2,128)(2,1)}), bf16[1024,2,768]{2,1,0:T(2,128)(2,1)}) %all-gather.11.cloned.1.call-update) | async-done | bytes 3145744 | tf_op jit(solution)/shard_map/all_gather | solution.py:107
  175.0 8.7 copy.56
  183.7 3.1 fusion
  186.8 1.7 exponential_reduce_fusion
  189.4 2.8 fusion.9
  192.2 1.8 copy.58
  194.3 19.9 %all-gather.13.cloned.1.call-done = bf16[768,768]{0,1:T(8,128)(2,1)} async-done(((bf16[768,48]{0,1:T(8,128)(2,1)}), bf16[768,768]{0,1:T(8,128)(2,1)}) %all-gather.13.cloned.1.call-update) | async-done | bytes 1179664 | tf_op jit(solution)/shard_map/all_gather | solution.py:87
  214.3 1.9 fusion.47
  216.4 52.4 %all-gather.15.cloned.1.call-done = bf16[768,3072]{0,1:T(8,128)(2,1)} async-done(((bf16[768,192]{0,1:T(8,128)(2,1)}), bf16[768,3072]{0,1:T(8,128)(2,1)}) %all-gather.15.cloned.1.call-update) | async-done | bytes 4718608 | tf_op jit(solution)/shard_map/all_gather | solution.py:88
  268.8 8.5 multiply_convert_fusion.1
  277.3 45.6 %all-gather.17.cloned.1.call-done = bf16[3072,768]{0,1:T(8,128)(2,1)} async-done(((bf16[3072,48]{0,1:T(8,128)(2,1)}), bf16[3072,768]{0,1:T(8,128)(2,1)}) %all-gather.17.cloned.1.call-update) | async-done | bytes 4718608 | tf_op jit(solution)/shard_map/all_gather | solution.py:89
  323.0 4.2 fusion.48
  328.2 1.5 convert_reduce_fusion.2
  329.7 2.1 convert_reduce_fusion
  331.8 1.5 multiply_reduce_fusion.2
  333.6 1.2 copy-done.5
  335.8 2.2 reshape.214
  338.0 2.5 copy.62
  340.5 8.7 multiply_reduce_fusion
  349.2 4.4 fusion.18
  353.6 2.0 fusion.22
  355.6 10.3 copy.64
  365.9 5.5 multiply_convert_fusion
  371.4 3.6 broadcast_multiply_fusion
  375.0 10.4 copy.63
  385.4 11.5 %pad_maximum_fusion = f32[1024,2,1536]{2,1,0:T(2,128)} fusion(f32[1024,2,768]{2,1,0:T(2,128)} %copy.64, f32[1024,2,768]{2,1,0:T(2,128)} %copy.63), kind=kLoop, calls=%fused_computation | loop fusion | flops 3145728 | bytes 25165824 | tf_op jit(solution)/shard_map/concatenate | solution.py:192
  397.0 273.8 %all-reduce.4 = bf16[1024,2,1536]{2,1,0:T(2,128)(2,1)} all-reduce(f32[1024,2,1536]{2,1,0:T(2,128)} %pad_maximum_fusion), channel_id=2, replica_groups=mesh['fsdp'=2,'ctx'=16] {'ctx'}, use_global_device_ids=true, to_apply=%region_11.12.clone | all-reduce | flops 3145728 | bytes 18874368
  670.8 4.4 convert_reduce_fusion.1
  675.8 1.1 dynamic-slice_convert_fusion.1
  677.0 1.9 convert_reduce_fusion.4
  679.9 4.1 convolution_bitcast_fusion
  685.1 5.1 fusion.35
  690.3 1.1 copy-done.7
  691.5 5.5 fusion.25
  697.8 78.4 %reduce-scatter.9.cloned.1.call-done = f32[3,768,48]{1,2,0:T(8,128)} async-done(((f32[3,768,768]{1,2,0:T(8,128)}), f32[3,768,48]{1,2,0:T(8,128)}) %reduce-scatter.9.cloned.1.call-update) | async-done | bytes 442384 | tf_op jit(solution)/shard_map/reduce_scatter | solution.py:221
  776.3 114.9 %reduce-scatter.17.cloned.1.call-done = f32[768,192]{0,1:T(8,128)} async-done(((f32[768,3072]{0,1:T(8,128)}), f32[768,192]{0,1:T(8,128)}) %reduce-scatter.17.cloned.1.call-update) | async-done | bytes 589840 | tf_op jit(solution)/shard_map/reduce_scatter | solution.py:223
  891.9 1.4 reduce_sum.184
  893.2 1.3 constant_dynamic-update-slice_fusion.3
  894.5 1.3 constant_dynamic-update-slice_fusion.11
  895.8 1.3 constant_dynamic-update-slice_fusion.10
  897.1 1.3 constant_dynamic-update-slice_fusion.9
  898.4 1.3 constant_dynamic-update-slice_fusion.8
  899.7 1.3 constant_dynamic-update-slice_fusion.7
  901.1 1.3 constant_dynamic-update-slice_fusion.6
  902.4 2.7 fusion.12
  905.2 101.6 %reduce-scatter.21.cloned.1.call-done = f32[3072,48]{0,1:T(8,128)} async-done(((f32[3072,768]{0,1:T(8,128)}), f32[3072,48]{0,1:T(8,128)}) %reduce-scatter.21.cloned.1.call-update) | async-done | bytes 589840 | tf_op jit(solution)/shard_map/reduce_scatter | solution.py:224
  1006.8 1.3 constant_dynamic-update-slice_fusion.5
  1008.1 1.7 convert_element_type.154
  1009.8 2.0 reshape.217
  1012.4 60.9 %all-reduce.2 = f32[9216]{0:T(1024)S(1)} all-reduce(f32[9216]{0:T(1024)} %constant_dynamic-update-slice_fusion.4), channel_id=11, replica_groups=mesh['fsdp'=2,'ctx'=16] {'ctx'}, use_global_device_ids=true, to_apply=%region_30.31.clone | all-reduce | flops 9216 | bytes 73728
  1073.4 4.9 psum.8
  1079.0 1.6 multiply_subtract_fusion.3
  1080.6 1.9 multiply_subtract_fusion.2
  1082.6 2.0 multiply_subtract_fusion.1
  1084.6 2.0 multiply_subtract_fusion
  (202 shorter events, 18.8 us)
Async XLA Ops:
  7.2 73.8 %all-gather.7.cloned.1.call-start = ((), (), s32[]{:S(2)}) async-start(), calls=%async_computation.8 | async-start | bytes 3760128 | tf_op jit(solution)/shard_map/all_gather | solution.py:86
  15.0 113.1 %all-gather.9.cloned.1.call-start = ((), (), s32[]{:S(2)}) async-start(), calls=%async_computation.9 | async-start | bytes 3342336 | tf_op jit(solution)/shard_map/all_gather | solution.py:108
  16.0 68.3 %copy-start.15 = (bf16[128,768,1]{1,0,2:T(8,128)(2,1)}, bf16[128,768,1]{1,0,2:T(8,128)(2,1)S(1)}, u32[]{:S(2)}) copy-start(bf16[128,768,1]{1,0,2:T(8,128)(2,1)S(1)} %reshape.224) | copy-start | bytes 589828
  80.4 22.9 %copy-start.35 = (f32[9216]{0:T(1024)}, f32[9216]{0:T(1024)S(1)}, u32[]{:S(2)}) copy-start(f32[9216]{0:T(1024)S(1)} %all-reduce) | copy-start | bytes 110596
  84.4 6.9 copy-start.17
  84.6 12.7 %copy-start.19 = (f32[1536,48]{0,1:T(8,128)S(1)}, f32[1536,48]{0,1:T(8,128)}, u32[]{:S(2)}) copy-start(f32[1536,48]{0,1:T(8,128)} %param.30) | copy-start | bytes 884740
  85.5 89.5 %all-gather.11.cloned.1.call-start = ((), (), s32[]{:S(2)}) async-start(), calls=%async_computation.10 | async-start | bytes 3342336 | tf_op jit(solution)/shard_map/all_gather | solution.py:107
  85.6 17.8 %copy-start.23 = (bf16[64,2,768]{2,1,0:T(2,128)(2,1)S(1)}, bf16[64,2,768]{2,1,0:T(2,128)(2,1)}, u32[]{:S(2)}) copy-start(bf16[64,2,768]{2,1,0:T(2,128)(2,1)} %param.18) | copy-start | bytes 589828
  86.3 17.8 %copy-start.24 = (bf16[64,2,768]{2,1,0:T(2,128)(2,1)S(1)}, bf16[64,2,768]{2,1,0:T(2,128)(2,1)}, u32[]{:S(2)}) copy-start(bf16[64,2,768]{2,1,0:T(2,128)(2,1)} %param.20) | copy-start | bytes 589828
  86.4 127.9 %all-gather.13.cloned.1.call-start = ((), (), s32[]{:S(2)}) async-start(), calls=%async_computation.11 | async-start | bytes 1253376 | tf_op jit(solution)/shard_map/all_gather | solution.py:87
  91.2 177.6 %all-gather.15.cloned.1.call-start = ((), (), s32[]{:S(2)}) async-start(), calls=%async_computation.12 | async-start | bytes 5013504 | tf_op jit(solution)/shard_map/all_gather | solution.py:88
  91.3 15.9 %copy-start.50 = (s32[2]{0:T(128)S(1)}, s32[2]{0:T(128)}, u32[]{:S(2)}) copy-start(s32[2]{0:T(128)} %param.19) | copy-start | bytes 28
  97.2 225.7 %all-gather.17.cloned.1.call-start = ((), (), s32[]{:S(2)}) async-start(), calls=%async_computation.13 | async-start | bytes 5013504 | tf_op jit(solution)/shard_map/all_gather | solution.py:89
  103.3 593.8 %reduce-scatter.13.cloned.1.call-start = ((), (), s32[]{:S(2)}) async-start(), calls=%async_computation.16 | async-start | bytes 2506752 | tf_op jit(solution)/shard_map/reduce_scatter | solution.py:222
  135.1 53.5 %copy-start.2 = (bf16[1024,2,768]{0,2,1:T(8,128)(2,1)}, bf16[1024,2,768]{0,2,1:T(8,128)(2,1)S(1)}, u32[]{:S(2)}) copy-start(bf16[1024,2,768]{0,2,1:T(8,128)(2,1)S(1)} %copy.55) | copy-start | bytes 9437188
  186.8 2.6 copy-start
  192.2 22.1 %copy-start.22 = (bf16[128,768]{1,0:T(8,128)(2,1)S(1)}, bf16[128,768]{1,0:T(8,128)(2,1)}, u32[]{:S(2)}) copy-start(bf16[128,768]{1,0:T(8,128)(2,1)} %reshape.211) | copy-start | bytes 589828
  192.2 22.1 %copy-start.40 = (f32[768]{0:T(1024)S(1)}, f32[768]{0:T(1024)}, u32[]{:S(2)}) copy-start(f32[768]{0:T(1024)} %get-tuple-element.55) | copy-start | bytes 9220
  194.0 74.8 %slice-start.6 = ((f32[9216]{0:T(1024)}), f32[3072]{0:T(1024)S(1)}, s32[]{:S(2)}) async-start(f32[9216]{0:T(1024)} %copy-done.35), calls=%async_computation.28 | async-start | bytes 24576 | tf_op jit(solution)/shard_map/slice | solution.py:100
  268.8 54.1 %copy-start.39 = (f32[768]{0:T(1024)S(1)}, f32[768]{0:T(1024)}, u32[]{:S(2)}) copy-start(f32[768]{0:T(1024)} %get-tuple-element.52) | copy-start | bytes 9220
  277.3 49.9 %copy-start.6 = (bf16[128,3072]{1,0:T(8,128)(2,1)}, bf16[128,3072]{1,0:T(8,128)(2,1)S(1)}, u32[]{:S(2)}) copy-start(bf16[128,3072]{1,0:T(8,128)(2,1)S(1)} %get-tuple-element.46) | copy-start | bytes 2359300
  322.9 6.8 slice-start.2
  322.9 4.5 copy-start.10
  322.9 5.3 copy-start.38
  322.9 5.3 copy-start.49
  323.0 6.7 slice-start.3
  323.0 6.7 copy-start.52
  327.2 2.5 copy-start.51
  328.2 3.6 slice-start.4
  333.6 20.1 %copy-start.4 = (f32[128,768]{1,0:T(8,128)}, f32[128,768]{1,0:T(8,128)S(1)}, u32[]{:S(2)}) copy-start(f32[128,768]{1,0:T(8,128)S(1)} %get-tuple-element.31) | copy-start | bytes 1179652
  334.8 5.7 copy-start.32
  335.8 13.4 %slice-start = ((s8[6291456]{0:T(1024)(128)(4,1)}), s8[2097152]{0:T(1024)(128)(4,1)S(1)}, s32[]{:S(2)}) async-start(s8[6291456]{0:T(1024)(128)(4,1)} %bitcast.49), calls=%async_computation.22 | async-start | bytes 4194304
  340.5 8.7 slice-start.1
  340.5 8.7 copy-start.9
  371.4 3.6 copy-start.3
  396.9 379.3 %reduce-scatter.9.cloned.1.call-start = ((), (), s32[]{:S(2)}) async-start(), calls=%async_computation.14 | async-start | bytes 7520256 | tf_op jit(solution)/shard_map/reduce_scatter | solution.py:221
  675.5 4.4 copy-start.16
  684.0 207.1 %reduce-scatter.17.cloned.1.call-start = ((), (), s32[]{:S(2)}) async-start(), calls=%async_computation.18 | async-start | bytes 10027008 | tf_op jit(solution)/shard_map/reduce_scatter | solution.py:223
  690.2 316.5 %reduce-scatter.21.cloned.1.call-start = ((), (), s32[]{:S(2)}) async-start(), calls=%async_computation.20 | async-start | bytes 10027008 | tf_op jit(solution)/shard_map/reduce_scatter | solution.py:224
  697.0 197.6 %copy-start.43 = (f32[768]{0:T(1024)S(1)}, f32[768]{0:T(1024)}, u32[]{:S(2)}) copy-start(f32[768]{0:T(1024)} %get-tuple-element.32) | copy-start | bytes 9220
  697.0 200.2 %copy-start.42 = (f32[768]{0:T(1024)S(1)}, f32[768]{0:T(1024)}, u32[]{:S(2)}) copy-start(f32[768]{0:T(1024)} %get-tuple-element.28) | copy-start | bytes 9220
  697.0 204.1 %copy-start.41 = (f32[768]{0:T(1024)S(1)}, f32[768]{0:T(1024)}, u32[]{:S(2)}) copy-start(f32[768]{0:T(1024)} %get-tuple-element.17) | copy-start | bytes 9220
  697.0 205.4 %copy-start.1 = (bf16[3,768,768]{1,2,0:T(8,128)(2,1)S(1)}, bf16[3,768,768]{1,2,0:T(8,128)(2,1)}, u32[]{:S(2)}) copy-start(bf16[3,768,768]{1,2,0:T(8,128)(2,1)} %all-gather.7.cloned.1.call-done) | copy-start | bytes 10616836
  697.0 382.0 %reduce-scatter.15.cloned.1.call-start = ((), (), s32[]{:S(2)}) async-start(), calls=%async_computation.17 | async-start | bytes 221184 | tf_op jit(solution)/shard_map/reduce_scatter | solution.py:229
  697.7 382.9 %reduce-scatter.11.cloned.1.call-start = ((), (), s32[]{:S(2)}) async-start(), calls=%async_computation.15 | async-start | bytes 663552 | tf_op jit(solution)/shard_map/reduce_scatter | solution.py:228
  776.2 306.4 %reduce-scatter.19.cloned.1.call-start = ((), (), s32[]{:S(2)}) async-start(), calls=%async_computation.19 | async-start | bytes 884736 | tf_op jit(solution)/shard_map/reduce_scatter | solution.py:230
  891.2 193.4 %reduce-scatter.23.cloned.1.call-start = ((), (), s32[]{:S(2)}) async-start(), calls=%async_computation.21 | async-start | bytes 884736 | tf_op jit(solution)/shard_map/reduce_scatter | solution.py:231
  902.4 104.4 %copy-start.45 = (f32[768]{0:T(1024)S(1)}, f32[768]{0:T(1024)}, u32[]{:S(2)}) copy-start(f32[768]{0:T(1024)} %get-tuple-element.23) | copy-start | bytes 9220
  905.1 106.8 %copy-start.46 = (f32[3072]{0:T(1024)S(1)}, f32[3072]{0:T(1024)}, u32[]{:S(2)}) copy-start(f32[3072]{0:T(1024)} %get-tuple-element.73) | copy-start | bytes 36868
  905.1 173.3 %copy-start.44 = (f32[576]{0:T(1024)S(1)}, f32[576]{0:T(1024)}, u32[]{:S(2)}) copy-start(f32[576]{0:T(1024)} %param.33) | copy-start | bytes 6916
  905.1 173.3 %copy-start.47 = (f32[576]{0:T(1024)S(1)}, f32[576]{0:T(1024)}, u32[]{:S(2)}) copy-start(f32[576]{0:T(1024)} %param.34) | copy-start | bytes 6916
  905.1 173.3 %copy-start.48 = (f32[576]{0:T(1024)S(1)}, f32[576]{0:T(1024)}, u32[]{:S(2)}) copy-start(f32[576]{0:T(1024)} %param.35) | copy-start | bytes 6916
  905.1 173.9 %copy-start.26 = (f32[384,48]{0,1:T(8,128)S(1)}, f32[384,48]{0,1:T(8,128)}, u32[]{:S(2)}) copy-start(f32[384,48]{0,1:T(8,128)} %param.24) | copy-start | bytes 221188
  905.1 173.9 %copy-start.36 = (f32[384,48]{0,1:T(8,128)S(1)}, f32[384,48]{0,1:T(8,128)}, u32[]{:S(2)}) copy-start(f32[384,48]{0,1:T(8,128)} %param.25) | copy-start | bytes 221188
  905.1 173.9 %copy-start.37 = (f32[384,48]{0,1:T(8,128)S(1)}, f32[384,48]{0,1:T(8,128)}, u32[]{:S(2)}) copy-start(f32[384,48]{0,1:T(8,128)} %param.26) | copy-start | bytes 221188
  905.1 175.5 %copy-start.21 = (f32[3,384,48]{1,2,0:T(8,128)S(1)}, f32[3,384,48]{1,2,0:T(8,128)}, u32[]{:S(2)}) copy-start(f32[3,384,48]{1,2,0:T(8,128)} %param.21) | copy-start | bytes 663556
  905.2 175.5 %copy-start.33 = (f32[3,384,48]{1,2,0:T(8,128)S(1)}, f32[3,384,48]{1,2,0:T(8,128)}, u32[]{:S(2)}) copy-start(f32[3,384,48]{1,2,0:T(8,128)} %param.22) | copy-start | bytes 663556
  905.2 175.5 %copy-start.34 = (f32[3,384,48]{1,2,0:T(8,128)S(1)}, f32[3,384,48]{1,2,0:T(8,128)}, u32[]{:S(2)}) copy-start(f32[3,384,48]{1,2,0:T(8,128)} %param.23) | copy-start | bytes 663556
  1009.8 72.8 %copy-start.18 = (f32[384,192]{0,1:T(8,128)S(1)}, f32[384,192]{0,1:T(8,128)}, u32[]{:S(2)}) copy-start(f32[384,192]{0,1:T(8,128)} %param.27) | copy-start | bytes 884740
  1009.8 72.8 %copy-start.27 = (f32[384,192]{0,1:T(8,128)S(1)}, f32[384,192]{0,1:T(8,128)}, u32[]{:S(2)}) copy-start(f32[384,192]{0,1:T(8,128)} %param.28) | copy-start | bytes 884740
  1009.8 72.8 %copy-start.28 = (f32[384,192]{0,1:T(8,128)S(1)}, f32[384,192]{0,1:T(8,128)}, u32[]{:S(2)}) copy-start(f32[384,192]{0,1:T(8,128)} %param.29) | copy-start | bytes 884740
  1080.6 4.0 copy-start.20
  1080.6 4.0 copy-start.29
  1080.6 4.0 copy-start.30
  (10 other events, 14.5 us)
Sparse Core Ops, SparseCore 0:
  15.1 49.4 all-gather.6
  85.6 42.4 all-gather.8
  130.9 43.9 all-gather.10
  177.1 37.1 all-gather.12
  216.4 52.3 all-gather.14
  271.0 51.9 all-gather.16
  397.1 76.4 reduce-scatter.12
  684.1 92.0 reduce-scatter.8
  780.3 110.8 reduce-scatter.16
  895.7 111.0 reduce-scatter.20
  1009.0 10.1 reduce-scatter.14
  1021.4 13.6 reduce-scatter.10
  1037.4 15.2 reduce-scatter.18
  1054.8 15.2 reduce-scatter.22
where the time goes:
time: 1100 us; the launch traced here: 1090 us
  waiting for transfers between devices  474 us (43%)
  blocking collectives  424 us (39%)
  local copies, waits for them, and re-layouts  74.2 us (7%)
  matrix products  68.9 us (6%)
  other arithmetic  34.6 us (3%)
  between operations  16.6 us (2%)
    unnamed x3, blocking collectives  396 us
    reduce_scatter x1, waiting for transfers between devices, on_device(): lax.psum_scatter(grad_expand, 'ctx', scatter_dimension=1, tiled=True)  115 us
    reduce_scatter x1, waiting for transfers between devices, on_device(): lax.psum_scatter(grad_contract, 'ctx', scatter_dimension=1, tiled=True)  102 us
    reduce_scatter x1, waiting for transfers between devices, on_device(): lax.psum_scatter(grad_attend, 'ctx', scatter_dimension=2, tiled=True)  78.4 us
    all_gather x1, waiting for transfers between devices, on_device(): lax.all_gather(row_tiles[2], 'ctx', axis=1, tiled=True)  52.4 us
    all_gather x1, waiting for transfers between devices, on_device(): lax.all_gather(row_tiles[3], 'ctx', axis=1, tiled=True)  45.6 us
    all_gather x1, waiting for transfers between devices, on_device(): lax.all_gather(local_keys, 'ctx', axis=0, tiled=True)  39.9 us
  transfers between devices with their start and end apart: 14, of which 8 were waited for; matrix products, arithmetic and copies ran while one was open for 8% of the time, Pallas kernels for 0%

commit v1 on v0

--- a/solution.py
+++ b/solution.py
@@ -1,8 +1,11 @@
+import functools
 import math
 
 import jax
 import jax.numpy as jnp
 from jax import lax
+from jax.experimental import pallas as pl
+from jax.experimental.pallas import tpu as pltpu
 from jax.sharding import PartitionSpec as P
 
 D = 768
@@ -52,6 +55,298 @@
         first_hat / (jnp.sqrt(second_hat) + ADAM_EPSILON) + decay * weight
     )
     return (new_weight, new_first, new_second)
+
+
+MESH = pl.DeviceIdType.MESH
+NZ, NY, NCORE = 4, 2, 2
+
+
+def place():
+    x = lax.axis_index("fsdp")
+    c = lax.axis_index("ctx")
+    return x, c // 4, (c // 2) % 2, c % 2
+
+
+def device_at(x, z, y, core):
+    return (x, z * 4 + y * 2 + core)
+
+
+def greet(partners):
+    barrier = pltpu.get_barrier_semaphore()
+    for partner in partners:
+        pl.semaphore_signal(barrier, inc=1, device_id=partner, device_id_type=MESH)
+    pl.semaphore_wait(barrier, len(partners))
+
+
+def partners_of(x, z, y, core, use_x):
+    found = [device_at(x, lax.rem(z + j, NZ), y, core) for j in range(1, NZ)]
+    found += [device_at(x, z, 1 - y, core), device_at(x, z, y, 1 - core)]
+    if use_x:
+        found.append(device_at(1 - x, z, y, core))
+    return found
+
+
+def gather_kernel(parts, use_x, own_ref, out_ref, local_sem, z_s, z_r, a_s, a_r, b_s, b_r, c_s, c_r):
+    x, z, y, core = place()
+    xi = x if use_x else 0
+    xo = 1 - x if use_x else 0
+    greet(partners_of(x, z, y, core, use_x))
+    core_peer = device_at(x, z, y, 1 - core)
+
+    def chunk(p, gx, gz, gy, gc):
+        start, rows, _ = parts[p]
+        return out_ref.at[gx, gz, gy, gc, pl.ds(start, rows)]
+
+    def copy(src, dst, send, recv, device):
+        return pltpu.make_async_remote_copy(
+            src_ref=src, dst_ref=dst, send_sem=send, recv_sem=recv, device_id=device, device_id_type=MESH
+        )
+
+    sent = []
+
+    def send(src, dst, send_sem, recv_sem, device):
+        item = copy(src, dst, send_sem, recv_sem, device)
+        item.start()
+        sent.append(item)
+
+    def landed(dst, send_sem, recv_sem):
+        copy(dst, dst, send_sem, recv_sem, core_peer).wait_recv()
+
+    local = pltpu.make_async_copy(own_ref, out_ref.at[xi, z, y, core], local_sem)
+    local.start()
+    axis = {"x": device_at(1 - x, z, y, core), "y": device_at(x, z, 1 - y, core)}
+
+    def flipped(p, gz, first, second):
+        order = parts[p][2]
+        gx, gy = xi, y
+        for flip, name in zip((first, second), order):
+            if flip and name == "x":
+                gx = xo
+            if flip and name == "y":
+                gy = 1 - y
+        return gx, gz, gy
+
+    def source(p, k):
+        start, rows, _ = parts[p]
+        if k == 0:
+            return own_ref.at[pl.ds(start, rows)]
+        return chunk(p, xi, lax.rem(z + k, NZ), y, core)
+
+    for p, (start, rows, order) in enumerate(parts):
+        for j in range(1, NZ):
+            send(
+                own_ref.at[pl.ds(start, rows)],
+                chunk(p, xi, z, y, core),
+                z_s.at[p, j - 1],
+                z_r.at[p, NZ - j - 1],
+                device_at(x, lax.rem(z + j, NZ), y, core),
+            )
+
+    def level_zero(p, k):
+        order = parts[p][2]
+        gz = lax.rem(z + k, NZ)
+        here = chunk(p, xi, gz, y, core)
+        if k > 0:
+            landed(here, z_s.at[p, k - 1], z_r.at[p, k - 1])
+        src = source(p, k)
+        send(src, here, a_s.at[p, k], a_r.at[p, k], axis[order[0]])
+        if len(order) > 1:
+            send(src, here, b_s.at[p, k, 0], b_r.at[p, k, 0], axis[order[1]])
+        send(src, here, c_s.at[p, k, 0], c_r.at[p, k, 0], core_peer)
+
+    def level_one(p, k):
+        order = parts[p][2]
+        gz = lax.rem(z + k, NZ)
+        here = chunk(p, *flipped(p, gz, True, False), core)
+        landed(here, a_s.at[p, k], a_r.at[p, k])
+        if len(order) > 1:
+            send(here, here, b_s.at[p, k, 1], b_r.at[p, k, 1], axis[order[1]])
+        send(here, here, c_s.at[p, k, 1], c_r.at[p, k, 1], core_peer)
+
+    def level_two(p, k):
+        if len(parts[p][2]) < 2:
+            return
+        gz = lax.rem(z + k, NZ)
+        for first in range(2):
+            here = chunk(p, *flipped(p, gz, first == 1, True), core)
+            landed(here, b_s.at[p, k, first], b_r.at[p, k, first])
+            send(here, here, c_s.at[p, k, 2 + first], c_r.at[p, k, 2 + first], core_peer)
+
+    for step in range(NZ + 2):
+        for level, work in enumerate((level_zero, level_one, level_two)):
+            k = step - level
+            if 0 <= k < NZ:
+                for p in range(len(parts)):
+                    work(p, k)
+    for k in range(NZ):
+        gz = lax.rem(z + k, NZ)
+        for p, (start, rows, order) in enumerate(parts):
+            for at in range(4 if len(order) > 1 else 2):
+                here = chunk(p, *flipped(p, gz, at % 2 == 1, at >= 2), 1 - core)
+                landed(here, c_s.at[p, k, at], c_r.at[p, k, at])
+    for item in sent:
+        item.wait_send()
+    local.wait()
+
+
+def gather_blocks(own, parts, use_x, collective_id):
+    n = len(parts)
+    dma = pltpu.SemaphoreType.DMA
+    return pl.pallas_call(
+        functools.partial(gather_kernel, parts, use_x),
+        out_shape=jax.ShapeDtypeStruct((2 if use_x else 1, NZ, NY, NCORE) + own.shape, own.dtype),
+        in_specs=[pl.BlockSpec(memory_space=pl.ANY)],
+        out_specs=pl.BlockSpec(memory_space=pl.ANY),
+        scratch_shapes=[dma]
+        + [dma((n, 3))] * 2
+        + [dma((n, NZ))] * 2
+        + [dma((n, NZ, 2))] * 2
+        + [dma((n, NZ, 4))] * 2,
+        compiler_params=pltpu.CompilerParams(collective_id=collective_id, has_side_effects=True),
+    )(own)
+
+
+def scatter_kernel(parts, use_x, g_ref, out_ref, r0, *rest):
+    n = len(parts)
+    ra, rb, rz = rest[:n], rest[n : 2 * n], rest[2 * n : 3 * n]
+    c_s, c_r, a_s, a_r, b_s, b_r, z_s, z_r = rest[3 * n :]
+    x, z, y, core = place()
+    nx = 2 if use_x else 1
+    xi = x if use_x else 0
+    xo = 1 - x if use_x else 0
+    greet(partners_of(x, z, y, core, use_x))
+    core_peer = device_at(x, z, y, 1 - core)
+    axis = {"x": device_at(1 - x, z, y, core), "y": device_at(x, z, 1 - y, core)}
+    sent = []
+
+    def copy(src, dst, send_sem, recv_sem, device):
+        return pltpu.make_async_remote_copy(
+            src_ref=src, dst_ref=dst, send_sem=send_sem, recv_sem=recv_sem, device_id=device, device_id_type=MESH
+        )
+
+    def send(src, dst, send_sem, recv_sem, device):
+        item = copy(src, dst, send_sem, recv_sem, device)
+        item.start()
+        sent.append(item)
+
+    def landed(dst, send_sem, recv_sem):
+        copy(dst, dst, send_sem, recv_sem, core_peer).wait_recv()
+
+    def added(one, two):
+        return (one.astype(jnp.float32) + two.astype(jnp.float32)).astype(jnp.bfloat16)
+
+    def goal(k):
+        return lax.rem(z + 1 + k, NZ)
+
+    for k in range(NZ):
+        for gx in range(nx):
+            send(g_ref.at[gx, goal(k), :, 1 - core], r0.at[k, gx], c_s.at[k, gx], c_r.at[k, gx], core_peer)
+
+    def level_zero(k):
+        for gx in range(nx):
+            landed(r0.at[k, gx], c_s.at[k, gx], c_r.at[k, gx])
+
+        @pl.loop(0, nx * NY)
+        def _(at):
+            gx, gy = at // NY, at % NY
+            r0[k, gx, gy] = added(r0[k, gx, gy], g_ref[gx, goal(k), gy, core])
+
+        for p, (start, rows, order) in enumerate(parts):
+            if order[0] == "x":
+                src = r0.at[k, xo, :, pl.ds(start, rows)]
+            else:
+                src = r0.at[k, :, 1 - y, pl.ds(start, rows)]
+            send(src, ra[p].at[k], a_s.at[p, k], a_r.at[p, k], axis[order[0]])
+
+    def level_one(k):
+        for p, (start, rows, order) in enumerate(parts):
+            landed(ra[p].at[k], a_s.at[p, k], a_r.at[p, k])
+            for other in range(ra[p].shape[1]):
+                if order[0] == "x":
+                    mine = r0[k, xi, other, pl.ds(start, rows)]
+                else:
+                    mine = r0[k, other, y, pl.ds(start, rows)]
+                ra[p][k, other] = added(ra[p][k, other], mine)
+            if len(order) > 1:
+                away = 1 - y if order[1] == "y" else 1 - x
+                send(ra[p].at[k, away], rb[p].at[k], b_s.at[p, k], b_r.at[p, k], axis[order[1]])
+            else:
+                last(p, k, ra[p].at[k, 0])
+
+    def level_two(k):
+        for p, (start, rows, order) in enumerate(parts):
+            if len(order) > 1:
+                landed(rb[p].at[k], b_s.at[p, k], b_r.at[p, k])
+                mine = ra[p][k, y if order[1] == "y" else x]
+                rb[p][k] = added(rb[p][k], mine)
+                last(p, k, rb[p].at[k])
+
+    def last(p, k, total):
+        if k < NZ - 1:
+            send(total, rz[p].at[k], z_s.at[p, k], z_r.at[p, k], device_at(x, goal(k), y, core))
+
+    for step in range(NZ + 2):
+        for level, work in enumerate((level_zero, level_one, level_two)):
+            k = step - level
+            if 0 <= k < NZ:
+                work(k)
+    for p, (start, rows, order) in enumerate(parts):
+        for k in range(NZ - 1):
+            landed(rz[p].at[k], z_s.at[p, k], z_r.at[p, k])
+        total = (rb[p][NZ - 1] if len(order) > 1 else ra[p][NZ - 1, 0]).astype(jnp.float32)
+        for k in range(NZ - 1):
+            total = total + rz[p][k].astype(jnp.float32)
+        out_ref[pl.ds(start, rows)] = total
+    for item in sent:
+        item.wait_send()
+
+
+def scatter_blocks(blocks, parts, use_x, collective_id):
+    n = len(parts)
+    rows, width = blocks.shape[-2:]
+    nx = blocks.shape[0]
+    dma = pltpu.SemaphoreType.DMA
+    low = jnp.bfloat16
+    return pl.pallas_call(
+        functools.partial(scatter_kernel, parts, use_x),
+        out_shape=jax.ShapeDtypeStruct((rows, width), jnp.float32),
+        in_specs=[pl.BlockSpec(memory_space=pltpu.VMEM)],
+        out_specs=pl.BlockSpec(memory_space=pltpu.VMEM),
+        scratch_shapes=[pltpu.VMEM((NZ, nx, NY, rows, width), low)]
+        + [pltpu.VMEM((NZ, NY if part[2][0] == "x" else nx, part[1], width), low) for part in parts]
+        + [pltpu.VMEM((NZ if len(part[2]) > 1 else 1, part[1], width), low) for part in parts]
+        + [pltpu.VMEM((NZ - 1, part[1], width), low) for part in parts]
+        + [dma((NZ, nx))] * 2
+        + [dma((n, NZ))] * 4
+        + [dma((n, NZ - 1))] * 2,
+        compiler_params=pltpu.CompilerParams(
+            collective_id=collective_id, has_side_effects=True, vmem_limit_bytes=48 * 1024 * 1024
+        ),
+    )(blocks)
+
+
+def halves(rows):
+    half = rows // 2
+    return ((0, half, ("y", "x")), (half, half, ("x", "y")))
+
+
+def halves_back(rows):
+    half = rows // 2
+    return ((0, half, ("x", "y")), (half, half, ("y", "x")))
+
+
+def split_three(values):
+    high = values.astype(jnp.bfloat16)
+    rest = values - high.astype(jnp.float32)
+    middle = rest.astype(jnp.bfloat16)
+    lowest = (rest - middle.astype(jnp.float32)).astype(jnp.bfloat16)
+    return jnp.stack([high, middle, lowest])
+
+
+def in_rows(values, lead, rows, width):
+    flat = values.reshape(lead + (-1,))
+    pad = [(0, 0)] * len(lead) + [(0, rows * width - flat.shape[-1])]
+    return jnp.pad(flat, pad).reshape(lead + (rows, width))
 
 
 def on_device(
@@ -76,19 +371,48 @@
 ):
     block, count, width = tokens.shape
     token_rows = block * count
-    row_tiles = (
-        lax.all_gather(attend_weight.astype(jnp.bfloat16), "fsdp", axis=1, tiled=True),
-        lax.all_gather(output_weight.astype(jnp.bfloat16), "fsdp", axis=0, tiled=True),
-        lax.all_gather(expand_weight.astype(jnp.bfloat16), "fsdp", axis=0, tiled=True),
-        lax.all_gather(contract_weight.astype(jnp.bfloat16), "fsdp", axis=0, tiled=True),
-    )
-    attend_full, output_full, expand_full, contract_full = (
-        lax.all_gather(row_tiles[0], "ctx", axis=2, tiled=True),
-        lax.all_gather(row_tiles[1], "ctx", axis=1, tiled=True),
-        lax.all_gather(row_tiles[2], "ctx", axis=1, tiled=True),
-        lax.all_gather(row_tiles[3], "ctx", axis=1, tiled=True),
-    )
-    vector = lax.all_gather(vector_params, "ctx", axis=0, tiled=True)
+    n_fsdp, n_ctx = lax.axis_size("fsdp"), lax.axis_size("ctx")
+    own_topology = (n_fsdp, n_ctx) == (2, NZ * NY * NCORE)
+    depth, wide = attend_weight.shape[1:]
+    wide_ff = expand_weight.shape[1]
+    folds = contract_weight.shape[0] // depth
+    nvec = vector_params.shape[0]
+    vec_rows = -(-3 * nvec // (depth * 32)) * 32
+    mat_rows = 3 * wide + wide + wide_ff + folds * wide
+    own = jnp.concatenate(
+        [
+            attend_weight.astype(jnp.bfloat16).transpose(0, 2, 1).reshape(3 * wide, depth),
+            output_weight.astype(jnp.bfloat16).T,
+            expand_weight.astype(jnp.bfloat16).T,
+            contract_weight.astype(jnp.bfloat16)
+            .reshape(folds, depth, wide)
+            .transpose(0, 2, 1)
+            .reshape(folds * wide, depth),
+            in_rows(split_three(vector_params), (), vec_rows, depth),
+        ]
+    )
+    if own_topology:
+        gathered = gather_blocks(own, halves(own.shape[0]), True, 1)
+    else:
+        gathered = lax.all_gather(own, ("fsdp", "ctx"))
+    gathered = gathered.reshape((n_fsdp, n_ctx) + own.shape)
+    at = 3 * wide
+    attend_back = (
+        gathered[:, :, :at].reshape(n_fsdp, n_ctx, 3, wide, depth).transpose(2, 1, 3, 0, 4).reshape(3, D, D)
+    )
+    output_back = gathered[:, :, at : at + wide].transpose(1, 2, 0, 3).reshape(D, D)
+    at += wide
+    expand_back = gathered[:, :, at : at + wide_ff].transpose(1, 2, 0, 3).reshape(FF, D)
+    at += wide_ff
+    contract_back = (
+        gathered[:, :, at : at + folds * wide]
+        .reshape(n_fsdp, n_ctx, folds, wide, depth)
+        .transpose(1, 3, 0, 2, 4)
+        .reshape(D, FF)
+    )
+    thirds = gathered[0, :, mat_rows:].reshape(n_ctx, -1)[:, : 3 * nvec].reshape(n_ctx, 3, nvec)
+    thirds = lax.optimization_barrier(thirds).astype(jnp.float32)
+    vector = ((thirds[:, 0] + thirds[:, 1]) + thirds[:, 2]).reshape(-1)
     bias_query = vector[0:D]
     bias_value = vector[D : 2 * D]
     bias_out = vector[2 * D : 3 * D]
@@ -99,14 +423,19 @@
     shift_two = vector[7 * D : 8 * D]
     bias_expand = vector[8 * D : 8 * D + FF]
     rows_in = tokens.reshape(token_rows, width)
-    proj = jnp.einsum("td,cde->cte", rows_in, attend_full, preferred_element_type=jnp.float32)
+    proj = jnp.einsum("td,ced->cte", rows_in, attend_back, preferred_element_type=jnp.float32)
     query = (proj[0] + bias_query).astype(jnp.bfloat16)
     local_keys = proj[1].astype(jnp.bfloat16).reshape(block, count, width)
     local_values = (proj[2] + bias_value).astype(jnp.bfloat16).reshape(block, count, width)
-    all_keys, all_values = (
-        lax.all_gather(local_keys, "ctx", axis=0, tiled=True),
-        lax.all_gather(local_values, "ctx", axis=0, tiled=True),
-    )
+    if own_topology:
+        both = jnp.stack([local_keys, local_values]).transpose(0, 2, 1, 3).reshape(2 * count * block, width)
+        both = gather_blocks(both, ((0, 2 * count * block, ("y",)),), False, 2)
+        both = both.reshape(n_ctx, 2, count, block, width)
+        all_keys = both[:, 0].transpose(0, 2, 1, 3).reshape(n_ctx * block, count, width)
+        all_values = both[:, 1].transpose(0, 2, 1, 3).reshape(n_ctx * block, count, width)
+    else:
+        all_keys = lax.all_gather(local_keys, "ctx", axis=0, tiled=True)
+        all_values = lax.all_gather(local_values, "ctx", axis=0, tiled=True)
     seq_len = all_keys.shape[0]
     valid = (jnp.arange(seq_len, dtype=jnp.int32)[None, :] < lengths[:, None])[:, None, None, :]
     scale = 1.0 / math.sqrt(HEAD_DIM)
@@ -129,15 +458,15 @@
         "shqk,kshd->qshd", probs_low, value_heads, preferred_element_type=jnp.float32
     )
     context = context.reshape(token_rows, width).astype(jnp.bfloat16)
-    attn = jnp.dot(context, output_full, preferred_element_type=jnp.float32) + bias_out
+    attn = jnp.einsum("te,de->td", context, output_back, preferred_element_type=jnp.float32) + bias_out
     mixed, normed_one, inverse_one = norm_parts(
         rows_in.astype(jnp.float32) + attn, gain_one, shift_one
     )
     mixed_low = mixed.astype(jnp.bfloat16)
-    pre = jnp.dot(mixed_low, expand_full, preferred_element_type=jnp.float32) + bias_expand
+    pre = jnp.einsum("td,fd->tf", mixed_low, expand_back, preferred_element_type=jnp.float32) + bias_expand
     act, gelu_back = jax.vjp(exact_gelu, pre)
     act_low = act.astype(jnp.bfloat16)
-    ffn = jnp.dot(act_low, contract_full, preferred_element_type=jnp.float32) + bias_contract
+    ffn = jnp.einsum("tf,df->td", act_low, contract_back, preferred_element_type=jnp.float32) + bias_contract
     layer_out, normed_two, inverse_two = norm_parts(mixed + ffn, gain_two, shift_two)
     grad_out = cotangent.reshape(token_rows, width).astype(jnp.float32)
     grad_gain_two = jnp.sum(grad_out * normed_two, axis=0)
@@ -145,13 +474,13 @@
     grad_resid = norm_back(grad_out, normed_two, inverse_two, gain_two)
     grad_ffn = grad_resid.astype(jnp.bfloat16)
     grad_bias_contract = jnp.sum(grad_ffn, axis=0, dtype=jnp.float32)
-    grad_contract = jnp.einsum("tf,td->fd", act_low, grad_ffn, preferred_element_type=jnp.float32)
-    grad_act = jnp.einsum("td,fd->tf", grad_ffn, contract_full, preferred_element_type=jnp.float32)
+    grad_contract = jnp.einsum("tf,td->df", act_low, grad_ffn, preferred_element_type=jnp.float32)
+    grad_act = jnp.einsum("td,df->tf", grad_ffn, contract_back, preferred_element_type=jnp.float32)
     grad_pre = gelu_back(grad_act)[0].astype(jnp.bfloat16)
     grad_bias_expand = jnp.sum(grad_pre, axis=0, dtype=jnp.float32)
-    grad_expand = jnp.einsum("td,tf->df", mixed_low, grad_pre, preferred_element_type=jnp.float32)
+    grad_expand = jnp.einsum("td,tf->fd", mixed_low, grad_pre, preferred_element_type=jnp.float32)
     grad_mixed = grad_resid + jnp.einsum(
-        "tf,df->td", grad_pre, expand_full, preferred_element_type=jnp.float32
+        "tf,fd->td", grad_pre, expand_back, preferred_element_type=jnp.float32
     )
     grad_gain_one = jnp.sum(grad_mixed * normed_one, axis=0)
     grad_shift_one = jnp.sum(grad_mixed, axis=0)
@@ -159,10 +488,10 @@
     grad_attn_low = grad_attn.astype(jnp.bfloat16)
     grad_bias_out = jnp.sum(grad_attn_low, axis=0, dtype=jnp.float32)
     grad_output = jnp.einsum(
-        "te,td->ed", context, grad_attn_low, preferred_element_type=jnp.float32
+        "te,td->de", context, grad_attn_low, preferred_element_type=jnp.float32
     )
     grad_context = jnp.einsum(
-        "td,ed->te", grad_attn_low, output_full, preferred_element_type=jnp.float32
+        "td,de->te", grad_attn_low, output_back, preferred_element_type=jnp.float32
     ).astype(jnp.bfloat16)
     key_rows, value_rows = (all_keys, all_values)
     probs_full = jnp.exp(masked_scores(key_rows) - log_total)
@@ -188,20 +517,32 @@
     grad_values = jnp.einsum(
         "shqk,qshd->kshd", probs_back, context_heads, preferred_element_type=jnp.float32
     )
-    summed = lax.psum_scatter(
-        jnp.concatenate(
-            [grad_keys.reshape(size, count, width), grad_values.reshape(size, count, width)], axis=2
-        ),
-        "ctx",
-        scatter_dimension=0,
-        tiled=True,
-    )
-    grad_keys_low = summed[:, :, :width].reshape(token_rows, width).astype(jnp.bfloat16)
-    grad_values_low = summed[:, :, width:].reshape(token_rows, width).astype(jnp.bfloat16)
+    if own_topology:
+        key_blocks = grad_keys.reshape(n_ctx, block, count, width).astype(jnp.bfloat16)
+        value_blocks = grad_values.reshape(n_ctx, block, count, width).astype(jnp.bfloat16)
+        blocks = jnp.stack([key_blocks, value_blocks], axis=1).transpose(0, 1, 3, 2, 4)
+        rows = 2 * count * block
+        summed = scatter_blocks(
+            blocks.reshape(1, NZ, NY, NCORE, rows, width), ((0, rows, ("y",)),), False, 3
+        )
+        summed = summed.astype(jnp.bfloat16).reshape(2, count, block, width).transpose(0, 2, 1, 3)
+        grad_keys_low = summed[0].reshape(token_rows, width)
+        grad_values_low = summed[1].reshape(token_rows, width)
+    else:
+        summed = lax.psum_scatter(
+            jnp.concatenate(
+                [grad_keys.reshape(size, count, width), grad_values.reshape(size, count, width)], axis=2
+            ),
+            "ctx",
+            scatter_dimension=0,
+            tiled=True,
+        )
+        grad_keys_low = summed[:, :, :width].reshape(token_rows, width).astype(jnp.bfloat16)
+        grad_values_low = summed[:, :, width:].reshape(token_rows, width).astype(jnp.bfloat16)
     stacked = jnp.stack([grad_query, grad_keys_low, grad_values_low])
-    grad_attend = jnp.einsum("td,cte->cde", rows_in, stacked, preferred_element_type=jnp.float32)
+    grad_attend = jnp.einsum("td,cte->ced", rows_in, stacked, preferred_element_type=jnp.float32)
     tokens_grad = grad_attn + jnp.einsum(
-        "cte,cde->td", stacked, attend_full, preferred_element_type=jnp.float32
+        "cte,ced->td", stacked, attend_back, preferred_element_type=jnp.float32
     )
     grad_vector = jnp.concatenate(
         [
@@ -216,21 +557,47 @@
             grad_bias_expand,
         ]
     )
-    vector_total = lax.psum(grad_vector, "fsdp")
-    column_parts = (
-        lax.psum_scatter(grad_attend, "ctx", scatter_dimension=2, tiled=True),
-        lax.psum_scatter(grad_output, "ctx", scatter_dimension=1, tiled=True),
-        lax.psum_scatter(grad_expand, "ctx", scatter_dimension=1, tiled=True),
-        lax.psum_scatter(grad_contract, "ctx", scatter_dimension=1, tiled=True),
-        lax.psum_scatter(vector_total, "ctx", scatter_dimension=0, tiled=True),
-    )
+    if own_topology:
+        cast = jnp.bfloat16
+    else:
+        cast = jnp.float32
+    lead = (n_fsdp, n_ctx)
+    vector_blocks = in_rows(grad_vector.astype(cast).reshape(n_ctx, nvec), (n_ctx,), vec_rows, depth)
+    blocks = jnp.concatenate(
+        [
+            grad_attend.astype(cast)
+            .reshape(3, n_ctx, wide, n_fsdp, depth)
+            .transpose(3, 1, 0, 2, 4)
+            .reshape(lead + (3 * wide, depth)),
+            grad_output.astype(cast).reshape(n_ctx, wide, n_fsdp, depth).transpose(2, 0, 1, 3),
+            grad_expand.astype(cast).reshape(n_ctx, wide_ff, n_fsdp, depth).transpose(2, 0, 1, 3),
+            grad_contract.astype(cast)
+            .reshape(n_ctx, wide, n_fsdp, folds, depth)
+            .transpose(2, 0, 3, 1, 4)
+            .reshape(lead + (folds * wide, depth)),
+            jnp.broadcast_to(vector_blocks, lead + (vec_rows, depth)),
+        ],
+        axis=2,
+    )
+    if own_topology:
+        total = scatter_blocks(
+            blocks.reshape((2, NZ, NY, NCORE) + own.shape), halves_back(own.shape[0]), True, 4
+        )
+    else:
+        total = lax.psum_scatter(
+            blocks.reshape((n_fsdp * n_ctx,) + own.shape), ("fsdp", "ctx"), scatter_dimension=0, tiled=True
+        ).reshape(own.shape)
+    at = 3 * wide
     owned = (
-        lax.psum_scatter(column_parts[0], "fsdp", scatter_dimension=1, tiled=True),
-        lax.psum_scatter(column_parts[1], "fsdp", scatter_dimension=0, tiled=True),
-        lax.psum_scatter(column_parts[2], "fsdp", scatter_dimension=0, tiled=True),
-        lax.psum_scatter(column_parts[3], "fsdp", scatter_dimension=0, tiled=True),
-    )
-    vector_owned = column_parts[4]
+        total[:at].reshape(3, wide, depth).transpose(0, 2, 1),
+        total[at : at + wide].T,
+        total[at + wide : at + wide + wide_ff].T,
+        total[at + wide + wide_ff : mat_rows]
+        .reshape(folds, wide, depth)
+        .transpose(0, 2, 1)
+        .reshape(folds * depth, wide),
+    )
+    vector_owned = total[mat_rows:].reshape(-1)[:nvec]
     attend_new = adam_step(
         attend_weight, attend_first, attend_second, owned[0], RATE_ATTEND, WEIGHT_DECAY
     )

time: 1100 us -> 650 us (0.59)
  waiting for transfers between devices: 474 us -> 0 us
  blocking collectives: 424 us -> 0 us
  Pallas kernels: 0 us -> 303 us
  local copies, waits for them, and re-layouts: 74.2 us -> 248 us
  matrix products: 68.9 us -> 52.1 us
  between operations: 16.6 us -> 2.06 us
    unnamed x3 -> x0, blocking collectives: 396 us -> none
    pallas_call x0 -> x4, Pallas kernels: none -> 303 us  [the longest x2 156 us: scatter_blocks(): pl.pallas_call(functools.partial(scatter_kernel, parts, use_x), out_shape...]
    reduce_scatter x8 -> x0, waiting for transfers between devices: 295 us -> none  [the longest x1 115 us: on_device(): lax.psum_scatter(grad_expand, 'ctx', scatter_dimension=1, tiled=True)]
    all_gather x6 -> x0, waiting for transfers between devices: 178 us -> none  [the longest x1 52.4 us: on_device(): lax.all_gather(row_tiles[2], 'ctx', axis=1, tiled=True)]
    reshape x2 -> x17, local copies, waits for them, and re-layouts: 20.7 us -> 63.1 us  [the longest x4 18.6 us: on_device(): blocks = jnp.concatenate([grad_attend.astype(cast).reshape(3, n_ctx, wide...]
    unnamed x132 -> x142, local copies, waits for them, and re-layouts: 17.9 us -> 52.3 us
    transpose x0 -> x5, local copies, waits for them, and re-layouts: none -> 30.4 us  [the longest x1 14.1 us: on_device(): jnp.stack([key_blocks, value_blocks], axis=1).transpose(0, 1, 3, 2, 4)]
    all_gather x4 -> x0, blocking collectives: 23.3 us -> none  [the longest x1 6.75 us: on_device(): lax.all_gather(attend_weight.astype(jnp.bfloat16), 'fsdp', axis=1, tiled=...]
  transfers between devices with their start and end apart: 14 -> 0, of which waited for: 8 -> 0; matrix products, arithmetic and copies ran while one was open for 8% -> 0% of each run, Pallas kernels for 0% -> 0%
where the time goes in v1:
time: 650 us; the launch traced here: 641 us
  Pallas kernels  303 us (47%)
  local copies, waits for them, and re-layouts  248 us (38%)
  matrix products  52.1 us (8%)
  other arithmetic  35.8 us (6%)
    pallas_call x2, Pallas kernels, scatter_blocks(): pl.pallas_call(functools.partial(scatter_kernel, parts, use_x), out_shape...  156 us
    pallas_call x2, Pallas kernels, gather_blocks(): pl.pallas_call(functools.partial(gather_kernel, parts, use_x), out_shape=...  147 us
    unnamed x142, local copies, waits for them, and re-layouts  52.3 us
    reshape x4, local copies, waits for them, and re-layouts, on_device(): blocks = jnp.concatenate([grad_attend.astype(cast).reshape(3, n_ctx, wide...  18.6 us
    reshape x2, local copies, waits for them, and re-layouts, on_device(): grad_expand.astype(cast).reshape(n_ctx, wide_ff, n_fsdp, depth)  15.9 us
    transpose x1, local copies, waits for them, and re-layouts, on_device(): jnp.stack([key_blocks, value_blocks], axis=1).transpose(0, 1, 3, 2, 4)  14.1 us
    reshape x2, local copies, waits for them, and re-layouts, on_device(): gathered[:, :, :at].reshape(n_fsdp, n_ctx, 3, wide, depth)  13.3 us

profile of v1, /device:TPU:0, one launch (start us, length us, event | category | flops | bytes accessed | tf_op | source)
XLA Modules:
  0.0 640.6 jit_solution(9603716228408062549)
XLA Ops:
  0.7 1.8 reduce.9
  12.3 82.3 %shard_map.305 = bf16[2,4,2,2,608,384]{5,4,3,2,1,0:T(8,128)(2,1)} custom-call(bf16[608,384]{1,0:T(8,128)(2,1)} %copy-done.23), custom_call_target="tpu_custom_call" | custom-call | tf_op jit(solution)/shard_map/pallas_call | solution.py:195
  101.8 2.4 slice.126
  104.2 6.9 %fusion.48 = (bf16[2,16,192,384]{3,2,1,0:T(8,128)(2,1)S(1)}, bf16[16,192,2,384]{3,1,0,2:T(8,128)(2,1)}) fusion(bf16[2,16,608,384]{3,2,1,0:T(8,128)(2,1)} %bitcast.150), kind=kLoop, calls=%fused_computation.135 | loop fusion | bytes 18874368 | tf_op jit(solution)/shard_map/slice | solution.py:408
  111.1 4.4 copy.89
  115.4 9.0 %reshape.329 = bf16[768,3072]{1,0:T(8,128)(2,1)} reshape(bf16[16,48,2,4,384]{4,3,2,1,0:T(4,128)(2,1)} %copy.89) | data formatting | bytes 9437184 | tf_op jit(solution)/shard_map/reshape | solution.py:411
  124.4 5.5 copy.117
  129.9 7.8 %reshape.322 = bf16[3,768,768]{2,1,0:T(8,128)(2,1)S(1)} reshape(bf16[3,16,48,2,384]{4,3,2,1,0:T(2,128)(2,1)} %bitcast.169) | data formatting | bytes 7077888 | tf_op jit(solution)/shard_map/reshape | solution.py:401
  137.7 2.2 convolution_bitcast_fusion
  144.9 2.0 squeeze.16
  147.9 1.7 pad_maximum_fusion
  149.7 2.3 squeeze.18
  151.9 2.1 add_convert_fusion.1
  154.0 2.2 copy.92
  156.3 9.3 %copy.88 = bf16[16,192,2,384]{3,2,1,0:T(2,128)(2,1)} copy(bf16[16,192,2,384]{3,1,0,2:T(8,128)(2,1)} %get-tuple-element.45) | data formatting | bytes 9437184 | tf_op jit(solution)/shard_map/transpose | solution.py:405
  165.6 5.3 copy.110
  170.9 64.9 %shard_map.306 = bf16[1,4,2,2,256,768]{5,4,3,2,1,0:T(8,128)(2,1)} custom-call(bf16[256,768]{1,0:T(8,128)(2,1)} %bitcast.174), custom_call_target="tpu_custom_call" | custom-call | tf_op jit(solution)/shard_map/pallas_call | solution.py:195
  235.9 6.2 fusion.49
  242.1 8.6 %copy.105 = bf16[16,1,2,64,768]{3,0,4,2,1:T(8,128)(2,1)} copy(bf16[16,1,2,64,768]{4,3,2,1,0:T(8,128)(2,1)} %get-tuple-element.46) | data formatting | bytes 6291456
  250.7 9.4 %reshape_reshape.10 = bf16[1024,2,12,64]{0,3,2,1:T(8,128)(2,1)} reshape(bf16[16,64,2,768]{1,0,3,2:T(8,128)(2,1)} %bitcast.152) | data formatting | bytes 6291456 | tf_op jit(solution)/shard_map/reshape;reshape | solution.py:445
  260.1 8.6 %copy.104 = bf16[16,1,2,64,768]{3,0,4,2,1:T(8,128)(2,1)} copy(bf16[16,1,2,64,768]{4,3,2,1,0:T(8,128)(2,1)} %get-tuple-element.47) | data formatting | bytes 6291456
  268.7 9.8 %reshape_reshape.4 = bf16[1024,2,12,64]{0,3,2,1:T(8,128)(2,1)} reshape(bf16[16,64,2,768]{1,0,3,2:T(8,128)(2,1)} %bitcast.153) | data formatting | bytes 6291456 | tf_op jit(solution)/shard_map/reshape;reshape | solution.py:456
  278.6 3.2 fusion
  286.0 2.7 fusion.10
  288.7 2.5 copy.86
  291.2 2.1 convert_element_type.219
  293.3 2.1 fusion.53
  295.7 6.7 %multiply_convert_fusion.2 = (bf16[128,3072]{1,0:T(8,128)(2,1)S(1)}, f32[128,3072]{1,0:T(8,128)S(1)}, f32[128,3072]{1,0:T(8,128)S(1)}) fusion(f32[3072]{0:T(1024)S(1)} %slice-done.8, bf16[3072,768]{1,0:T(8,128)(2,1)} %bitcast.157, f32[128,768]{1,0:T(8,128)S(1)} %get-tuple-element.67, f32[768]{0:T(1024)} %get-tuple-element.57, f32[768]{0:T(1024)} %get-tuple-element.58, ...), kind=kOutput, calls=%fused_computation.20 | convolution fusion | flops 630423552 | bytes 9063424 | tf_op jit(solution)/shard_map/td,fd->tf/dot_general | solution.py:466
  302.5 1.8 fusion.54
  305.6 2.1 fusion.56
  312.8 2.1 reshape.330
  314.9 2.2 copy.93
  317.1 2.6 convolution_convert_fusion.3
  319.7 3.6 reshape.335
  323.3 2.6 copy.99
  325.9 6.6 %convert_bitcast_fusion = bf16[1024,2,12,64]{0,3,2,1:T(8,128)(2,1)} fusion(bf16[64,2,12,64]{0,3,2,1:T(8,128)(2,1)} %copy.93, f32[2,12,64,1024]{3,2,1,0:T(8,128)} %copy-done, f32[2,12,64]{2,1,0:T(8,128)} %copy-done.29, pred[2,1024]{1,0:T(4,128)(4,1)S(1)} %iota_compare_fusion), kind=kOutput, calls=%fused_computation.15 | convolution fusion | flops 209190912 | bytes 9641984 | tf_op jit(solution)/shard_map/shqk,qshd->kshd/dot_general | solution.py:517
  332.6 2.5 multiply_reduce_fusion
  335.0 1.7 multiply_convert_fusion.1
  336.9 2.3 fusion.55
  339.3 2.7 fusion.2
  344.3 2.1 copy.91
  346.4 2.1 convert_element_type.234
  350.0 9.2 %convert_element_type.237 = bf16[16,1,64,2,768]{2,0,4,3,1:T(8,128)(2,1)} reshape(bf16[1024,2,12,64]{0,3,2,1:T(8,128)(2,1)} %fusion.2) | data formatting | bytes 6291456 | tf_op jit(solution)/shard_map/convert_element_type | solution.py:521
  359.2 9.2 %convert_element_type.240 = bf16[16,1,64,2,768]{2,0,4,3,1:T(8,128)(2,1)} reshape(bf16[1024,2,12,64]{0,3,2,1:T(8,128)(2,1)} %convert_bitcast_fusion) | data formatting | bytes 6291456 | tf_op jit(solution)/shard_map/convert_element_type | solution.py:522
  368.5 11.2 %maximum_bitcast_fusion = bf16[16,2,2,64,768]{3,0,4,2,1:T(8,128)(2,1)} fusion(bf16[16,1,64,2,768]{2,0,4,3,1:T(8,128)(2,1)} %convert_element_type.240, bf16[16,1,64,2,768]{2,0,4,3,1:T(8,128)(2,1)} %convert_element_type.237), kind=kLoop, calls=%fused_computation | loop fusion | flops 3145728 | bytes 12582912 | tf_op jit(solution)/shard_map/transpose | solution.py:523
  379.7 14.1 %copy.94 = bf16[16,2,2,64,768]{4,3,2,1,0:T(8,128)(2,1)} copy(bf16[16,2,2,64,768]{3,0,4,2,1:T(8,128)(2,1)} %maximum_bitcast_fusion) | data formatting | bytes 12582912 | tf_op jit(solution)/shard_map/transpose | solution.py:523
  393.7 68.9 %shard_map.307 = f32[256,768]{1,0:T(8,128)S(1)} custom-call(bf16[1,4,2,2,256,768]{5,4,3,2,1,0:T(8,128)(2,1)} %bitcast.154), custom_call_target="tpu_custom_call" | custom-call | tf_op jit(solution)/shard_map/pallas_call | solution.py:310
  476.7 1.8 copy.96
  480.2 1.8 copy.95
  486.9 2.6 fusion.13
  489.5 2.0 reshape.333
  493.0 2.2 convolution_convert_fusion.2
  495.2 3.1 reshape.334
  498.4 2.5 copy.98
  501.0 3.7 convolution_convert_fusion.1
  504.7 10.3 %reshape.336 = bf16[16,192,2,384]{3,2,1,0:T(2,128)(2,1)} reshape(bf16[3072,768]{1,0:T(8,128)(2,1)} %convolution_convert_fusion.1) | data formatting | bytes 9437184 | tf_op jit(solution)/shard_map/reshape | solution.py:573
  515.0 5.5 copy.100
  520.5 3.6 convolution_convert_fusion
  524.1 9.6 %reshape.337 = bf16[16,48,2,4,384]{4,3,2,1,0:T(4,128)(2,1)} reshape(bf16[768,3072]{1,0:T(8,128)(2,1)} %convolution_convert_fusion) | data formatting | bytes 9437184 | tf_op jit(solution)/shard_map/reshape | solution.py:575
  533.8 3.3 copy.101
  537.0 2.2 constant_dynamic-update-slice_fusion.9
  541.4 2.6 constant_dynamic-update-slice_fusion.7
  544.0 2.7 constant_dynamic-update-slice_fusion.6
  547.8 86.8 %shard_map.308 = f32[608,384]{1,0:T(8,128)S(1)} custom-call(bf16[2,4,2,2,608,384]{5,4,3,2,1,0:T(8,128)(2,1)} %broadcast_dynamic-update-slice_fusion.g_ref), custom_call_target="tpu_custom_call" | custom-call | tf_op jit(solution)/shard_map/pallas_call | solution.py:310
  (217 shorter events, 68.6 us)
Async XLA Ops:
  0.7 10.7 %copy-start.18 = (bf16[64,2,768]{2,1,0:T(2,128)(2,1)S(1)}, bf16[64,2,768]{2,1,0:T(2,128)(2,1)}, u32[]{:S(2)}) copy-start(bf16[64,2,768]{2,1,0:T(2,128)(2,1)} %param.20) | copy-start | bytes 589828
  11.4 0.9 copy-start.23
  96.3 5.6 copy-start.33
  96.9 5.0 copy-start.37
  97.9 3.9 copy-start.36
  140.0 12.0 %slice-start.9 = ((f32[144,64]{1,0:T(8,128)}), f32[12,64]{1,0:T(8,128)S(1)}, s32[]{:S(2)}) async-start(f32[144,64]{1,0:T(8,128)} %copy-done.36), calls=%async_computation.9 | async-start | bytes 16384 | tf_op jit(solution)/shard_map/slice | solution.py:416
  281.8 3.2 copy-start
  281.8 4.2 copy-start.3
  285.0 0.6 copy-start.29
  288.7 6.9 %slice-start.8 = ((f32[9216]{0:T(1024)}), f32[3072]{0:T(1024)S(1)}, s32[]{:S(2)}) async-start(f32[9216]{0:T(1024)} %copy-done.33), calls=%async_computation.8 | async-start | bytes 24576 | tf_op jit(solution)/shard_map/slice | solution.py:424
  293.3 9.1 %slice-start.2 = ((s8[4718592]{0:T(1024)(128)(4,1)}), s8[4194304]{0:T(1024)(128)(4,1)S(1)}, s32[]{:S(2)}) async-start(s8[4718592]{0:T(1024)(128)(4,1)} %bitcast.155), calls=%async_computation.2 | async-start | bytes 8388608
  295.4 13.9 %copy-start.1 = (f32[128,768]{1,0:T(8,128)}, f32[128,768]{1,0:T(8,128)S(1)}, u32[]{:S(2)}) copy-start(f32[128,768]{1,0:T(8,128)S(1)} %get-tuple-element.67) | copy-start | bytes 1179652
  295.4 13.9 %copy-start.44 = (f32[128]{0:T(128)}, f32[128]{0:T(128)S(1)}, u32[]{:S(2)}) copy-start(f32[128]{0:T(128)S(1)} %broadcast_multiply_fusion.5) | copy-start | bytes 1540
  295.7 13.7 %copy-start.46 = (f32[128]{0:T(128)}, f32[128]{0:T(128)S(1)}, u32[]{:S(2)}) copy-start(f32[128]{0:T(128)S(1)} %add_rsqrt_fusion.1) | copy-start | bytes 1540
  295.7 6.7 %slice-start.3 = ((s8[4718592]{0:T(1024)(128)(4,1)}), s8[524288]{0:T(1024)(128)(4,1)S(1)}, s32[]{:S(2)}) async-start(s8[4718592]{0:T(1024)(128)(4,1)} %bitcast.155), calls=%async_computation.3 | async-start | bytes 1048576
  295.7 6.7 %copy-start.34 = (f32[768]{0:T(1024)S(1)}, f32[768]{0:T(1024)}, u32[]{:S(2)}) copy-start(f32[768]{0:T(1024)} %get-tuple-element.58) | copy-start | bytes 9220
  295.7 6.7 %copy-start.39 = (f32[768]{0:T(1024)S(1)}, f32[768]{0:T(1024)}, u32[]{:S(2)}) copy-start(f32[768]{0:T(1024)} %get-tuple-element.57) | copy-start | bytes 9220
  295.7 6.7 %copy-start.42 = (f32[768]{0:T(1024)S(1)}, f32[768]{0:T(1024)}, u32[]{:S(2)}) copy-start(f32[768]{0:T(1024)} %get-tuple-element.56) | copy-start | bytes 9220
  302.4 1.9 copy-start.16
  302.5 2.0 copy-start.15
  302.5 2.0 copy-start.38
  302.5 2.0 copy-start.41
  302.5 2.9 copy-start.51
  304.5 3.3 slice-start.4
  305.6 2.2 copy-start.10
  305.6 2.2 slice-start.5
  307.8 1.5 copy-start.7
  307.8 2.3 copy-start.6
  310.1 1.0 copy-start.9
  323.3 9.3 %slice-start = ((s8[6291456]{0:T(1024)(128)(4,1)}), s8[4194304]{0:T(1024)(128)(4,1)S(1)}, s32[]{:S(2)}) async-start(s8[6291456]{0:T(1024)(128)(4,1)} %bitcast.145), calls=%async_computation | async-start | bytes 8388608
  325.9 6.6 %slice-start.1 = ((s8[6291456]{0:T(1024)(128)(4,1)}), s8[2097152]{0:T(1024)(128)(4,1)S(1)}, s32[]{:S(2)}) async-start(s8[6291456]{0:T(1024)(128)(4,1)} %bitcast.145), calls=%async_computation.1 | async-start | bytes 4194304
  325.9 6.6 %copy-start.4 = (bf16[1024,2,12,64]{0,3,2,1:T(8,128)(2,1)S(1)}, bf16[1024,2,12,64]{0,3,2,1:T(8,128)(2,1)}, u32[]{:S(2)}) copy-start(bf16[1024,2,12,64]{0,3,2,1:T(8,128)(2,1)} %reshape_reshape.4) | copy-start | bytes 9437188
  325.9 6.6 %copy-start.14 = (bf16[64,2,12,64]{0,3,2,1:T(8,128)(2,1)S(1)}, bf16[64,2,12,64]{0,3,2,1:T(8,128)(2,1)}, u32[]{:S(2)}) copy-start(bf16[64,2,12,64]{0,3,2,1:T(8,128)(2,1)} %copy.93) | copy-start | bytes 589828
  325.9 6.6 %copy-start.30 = (f32[2,12,64]{2,1,0:T(8,128)S(1)}, f32[2,12,64]{2,1,0:T(8,128)}, u32[]{:S(2)}) copy-start(f32[2,12,64]{2,1,0:T(8,128)} %copy-done.29) | copy-start | bytes 18436
  335.0 1.9 copy-start.5
  336.9 2.3 copy-start.13
  393.7 78.8 %copy-start.48 = (bf16[768]{0:T(1024)(128)(2,1)S(1)}, bf16[768]{0:T(1024)(128)(2,1)}, u32[]{:S(2)}) copy-start(bf16[768]{0:T(1024)(128)(2,1)} %reduce.9) | copy-start | bytes 4612
  498.4 2.6 copy-start.2
  498.4 2.6 copy-start.8
  498.4 2.6 copy-start.35
  498.4 2.6 copy-start.40
  498.4 2.6 copy-start.45
  498.4 2.6 copy-start.47
  515.0 5.5 copy-start.11
  515.0 5.5 copy-start.17
  537.0 4.2 slice-start.6
  537.0 2.2 copy-start.12
  537.0 4.3 slice-start.7
  544.0 2.7 copy-start.19
  547.7 87.0 %copy-start.43 = (f32[576]{0:T(1024)S(1)}, f32[576]{0:T(1024)}, u32[]{:S(2)}) copy-start(f32[576]{0:T(1024)} %param.33) | copy-start | bytes 6916
  547.7 87.0 %copy-start.49 = (f32[576]{0:T(1024)S(1)}, f32[576]{0:T(1024)}, u32[]{:S(2)}) copy-start(f32[576]{0:T(1024)} %param.34) | copy-start | bytes 6916
  547.7 87.0 %copy-start.50 = (f32[576]{0:T(1024)S(1)}, f32[576]{0:T(1024)}, u32[]{:S(2)}) copy-start(f32[576]{0:T(1024)} %param.35) | copy-start | bytes 6916
  547.7 87.6 %copy-start.24 = (f32[384,48]{0,1:T(8,128)S(1)}, f32[384,48]{0,1:T(8,128)}, u32[]{:S(2)}) copy-start(f32[384,48]{0,1:T(8,128)} %param.24) | copy-start | bytes 221188
  547.7 89.3 %copy-start.20 = (f32[384,192]{0,1:T(8,128)S(1)}, f32[384,192]{0,1:T(8,128)}, u32[]{:S(2)}) copy-start(f32[384,192]{0,1:T(8,128)} %param.27) | copy-start | bytes 884740
  547.7 89.3 %copy-start.25 = (f32[384,192]{0,1:T(8,128)S(1)}, f32[384,192]{0,1:T(8,128)}, u32[]{:S(2)}) copy-start(f32[384,192]{0,1:T(8,128)} %param.28) | copy-start | bytes 884740
  547.7 89.3 %copy-start.26 = (f32[384,192]{0,1:T(8,128)S(1)}, f32[384,192]{0,1:T(8,128)}, u32[]{:S(2)}) copy-start(f32[384,192]{0,1:T(8,128)} %param.29) | copy-start | bytes 884740
  634.6 3.5 copy-start.22
  634.6 3.5 copy-start.31
  634.6 3.5 copy-start.32
  634.6 4.5 copy-start.21
  634.6 4.5 copy-start.27
  634.6 4.4 copy-start.28

commit v2 on v0

v2 whole, which is shorter than its diff:
```python
import functools
import math

import jax
import jax.numpy as jnp
from jax import lax
from jax.experimental import pallas as pl
from jax.experimental.pallas import tpu as pltpu
from jax.sharding import PartitionSpec as P

D = 768
HEADS = 12
HEAD_DIM = 64
FF = 3072
STEP = 10


NORM_EPSILON = 1e-06
MASK_FILL = -1e30
BETA_ONE = 0.9
BETA_TWO = 0.999
ADAM_EPSILON = 1e-08
WEIGHT_DECAY = 0.01
RATE_ATTEND = 0.08
RATE_OUTPUT = 0.2
RATE_EXPAND = 0.05
RATE_CONTRACT = 0.025
RATE_VECTOR = 0.3


def norm_parts(values, gain, shift):
    centre = values - jnp.mean(values, axis=-1, keepdims=True)
    spread = jnp.mean(centre * centre, axis=-1, keepdims=True)
    inverse = lax.rsqrt(spread + NORM_EPSILON)
    normed = centre * inverse
    return (normed * gain + shift, normed, inverse)


def norm_back(grad_out, normed, inverse, gain):
    scaled = grad_out * gain
    centred = scaled - jnp.mean(scaled, axis=-1, keepdims=True)
    return inverse * (centred - normed * jnp.mean(scaled * normed, axis=-1, keepdims=True))


def exact_gelu(values):
    return jax.nn.gelu(values, approximate=False)


def adam_step(weight, first, second, grad, rate, decay):
    new_first = BETA_ONE * first + (1.0 - BETA_ONE) * grad
    new_second = BETA_TWO * second + (1.0 - BETA_TWO) * grad * grad
    first_hat = new_first / (1.0 - BETA_ONE**STEP)
    second_hat = new_second / (1.0 - BETA_TWO**STEP)
    new_weight = weight - rate * (
        first_hat / (jnp.sqrt(second_hat) + ADAM_EPSILON) + decay * weight
    )
    return (new_weight, new_first, new_second)


MESH = pl.DeviceIdType.MESH
NZ, NY, NCORE = 4, 2, 2


def place():
    x = lax.axis_index("fsdp")
    c = lax.axis_index("ctx")
    return x, c // 4, (c // 2) % 2, c % 2


def device_at(x, z, y, core):
    return (x, z * 4 + y * 2 + core)


def greet(partners):
    barrier = pltpu.get_barrier_semaphore()
    for partner in partners:
        pl.semaphore_signal(barrier, inc=1, device_id=partner, device_id_type=MESH)
    pl.semaphore_wait(barrier, len(partners))


def partners_of(x, z, y, core, use_x):
    found = [device_at(x, lax.rem(z + j, NZ), y, core) for j in range(1, NZ)]
    found += [device_at(x, z, 1 - y, core), device_at(x, z, y, 1 - core)]
    if use_x:
        found.append(device_at(1 - x, z, y, core))
    return found


def remote(src, dst, send_sem, recv_sem, device):
    return pltpu.make_async_remote_copy(
        src_ref=src, dst_ref=dst, send_sem=send_sem, recv_sem=recv_sem, device_id=device, device_id_type=MESH
    )


def lanes(at, width):
    return pl.ds(pl.multiple_of(at * width, 128), width)


def gather_kernel(orders, use_x, *refs):
    n = len(orders)
    own_refs, out_refs = refs[:n], refs[n : 2 * n]
    local_sem, z_s, z_r, a_s, a_r, b_s, b_r, c_s, c_r = refs[2 * n :]
    x, z, y, core = place()
    greet(partners_of(x, z, y, core, use_x))
    core_peer = device_at(x, z, y, 1 - core)
    axis = {"x": device_at(1 - x, z, y, core), "y": device_at(x, z, 1 - y, core)}
    sent = []

    def chunk(p, gx, gz, gy, gc):
        out, c = out_refs[p], gz * 4 + gy * 2 + gc
        if not use_x:
            return out.at[c]
        half = lanes(gx, own_refs[p].shape[-1])
        return out.at[:, c, :, half] if len(out.shape) == 4 else out.at[c, :, half]

    def send(src, dst, send_sem, recv_sem, device):
        item = remote(src, dst, send_sem, recv_sem, device)
        item.start()
        sent.append(item)

    def landed(dst, send_sem, recv_sem):
        remote(dst, dst, send_sem, recv_sem, core_peer).wait_recv()

    def flipped(p, gz, first, second, gc):
        gx, gy = x, y
        for flip, name in zip((first, second), orders[p]):
            if flip and name == "x":
                gx = 1 - x
            if flip and name == "y":
                gy = 1 - y
        return chunk(p, gx, gz, gy, gc)

    local = [pltpu.make_async_copy(own_refs[p], chunk(p, x, z, y, core), local_sem.at[p]) for p in range(n)]
    for p in range(n):
        for j in range(1, NZ):
            there = device_at(x, lax.rem(z + j, NZ), y, core)
            send(own_refs[p], chunk(p, x, z, y, core), z_s.at[p, j - 1], z_r.at[p, NZ - j - 1], there)

    def level_zero(p, k):
        here = chunk(p, x, lax.rem(z + k, NZ), y, core)
        if k > 0:
            landed(here, z_s.at[p, k - 1], z_r.at[p, k - 1])
        src = here if k > 0 else own_refs[p]
        send(src, here, a_s.at[p, k], a_r.at[p, k], axis[orders[p][0]])
        if len(orders[p]) > 1:
            send(src, here, b_s.at[p, k, 0], b_r.at[p, k, 0], axis[orders[p][1]])
        send(src, here, c_s.at[p, k, 0], c_r.at[p, k, 0], core_peer)

    def level_one(p, k):
        here = flipped(p, lax.rem(z + k, NZ), True, False, core)
        landed(here, a_s.at[p, k], a_r.at[p, k])
        if len(orders[p]) > 1:
            send(here, here, b_s.at[p, k, 1], b_r.at[p, k, 1], axis[orders[p][1]])
        send(here, here, c_s.at[p, k, 1], c_r.at[p, k, 1], core_peer)

    def level_two(p, k):
        if len(orders[p]) < 2:
            return
        for first in range(2):
            here = flipped(p, lax.rem(z + k, NZ), first == 1, True, core)
            landed(here, b_s.at[p, k, first], b_r.at[p, k, first])
            send(here, here, c_s.at[p, k, 2 + first], c_r.at[p, k, 2 + first], core_peer)

    for step in range(NZ + 2):
        for level, work in enumerate((level_zero, level_one, level_two)):
            k = step - level
            if 0 <= k < NZ:
                for p in range(n):
                    work(p, k)
        if step == 0:
            for item in local:
                item.start()
    for k in range(NZ):
        for p in range(n):
            for at in range(4 if len(orders[p]) > 1 else 2):
                here = flipped(p, lax.rem(z + k, NZ), at % 2 == 1, at >= 2, 1 - core)
                landed(here, c_s.at[p, k, at], c_r.at[p, k, at])
    for item in sent:
        item.wait_send()
    for item in local:
        item.wait()


def gather_blocks(owns, orders, use_x, collective_id):
    n = len(orders)
    dma = pltpu.SemaphoreType.DMA
    count = NZ * NY * NCORE
    times = 2 if use_x else 1
    shapes = [o.shape[:-2] + (count, o.shape[-2], o.shape[-1] * times) for o in owns]
    anywhere = pl.BlockSpec(memory_space=pl.ANY)
    return pl.pallas_call(
        functools.partial(gather_kernel, orders, use_x),
        out_shape=[jax.ShapeDtypeStruct(s, o.dtype) for s, o in zip(shapes, owns)],
        in_specs=[anywhere] * n,
        out_specs=[anywhere] * n,
        scratch_shapes=[dma((n,))]
        + [dma((n, 3))] * 2
        + [dma((n, NZ))] * 2
        + [dma((n, NZ, 2))] * 2
        + [dma((n, NZ, 4))] * 2,
        compiler_params=pltpu.CompilerParams(collective_id=collective_id, has_side_effects=True),
    )(*owns)


def scatter_kernel(orders, use_x, *refs):
    n = len(orders)
    g, out = refs[:n], refs[n : 2 * n]
    r0, ra, rb, rz = (refs[i * n : (i + 1) * n] for i in range(2, 6))
    c_s, c_r, a_s, a_r, b_s, b_r, z_s, z_r = refs[6 * n :]
    x, z, y, core = place()
    greet(partners_of(x, z, y, core, use_x))
    core_peer = device_at(x, z, y, 1 - core)
    axis = {"x": device_at(1 - x, z, y, core), "y": device_at(x, z, 1 - y, core)}
    sent = []

    def send(src, dst, send_sem, recv_sem, device):
        item = remote(src, dst, send_sem, recv_sem, device)
        item.start()
        sent.append(item)

    def landed(dst, send_sem, recv_sem):
        remote(dst, dst, send_sem, recv_sem, core_peer).wait_recv()

    def added(one, two):
        return (one.astype(jnp.float32) + two.astype(jnp.float32)).astype(jnp.bfloat16)

    def goal(k):
        return lax.rem(z + 1 + k, NZ)

    def mine(p, k, gy, gc):
        c = goal(k) * 4 + gy * 2 + gc
        return g[p].at[:, c] if len(g[p].shape) == 4 else g[p].at[c]

    def half(p, gx):
        return lanes(gx, out[p].shape[-1])

    def columns(p, ref, gx):
        return ref.at[(slice(None),) * (len(ref.shape) - 1) + (half(p, gx),)]

    for k in range(NZ):
        for p in range(n):
            for gy in range(NY):
                send(mine(p, k, gy, 1 - core), r0[p].at[k, gy], c_s.at[p, k, gy], c_r.at[p, k, gy], core_peer)

    def level_zero(p, k):
        for gy in range(NY):
            landed(r0[p].at[k, gy], c_s.at[p, k, gy], c_r.at[p, k, gy])

        @pl.loop(0, NY)
        def _(gy):
            r0[p][k, gy] = added(r0[p][k, gy], mine(p, k, gy, core)[...])

        src = columns(p, r0[p].at[k], 1 - x) if orders[p][0] == "x" else r0[p].at[k, 1 - y]
        send(src, ra[p].at[k], a_s.at[p, k], a_r.at[p, k], axis[orders[p][0]])

    def level_one(p, k):
        landed(ra[p].at[k], a_s.at[p, k], a_r.at[p, k])
        kept = columns(p, r0[p].at[k], x) if orders[p][0] == "x" else r0[p].at[k, y]
        ra[p][k] = added(ra[p][k], kept[...])
        if len(orders[p]) > 1:
            src = columns(p, ra[p].at[k], 1 - x) if orders[p][1] == "x" else ra[p].at[k, 1 - y]
            send(src, rb[p].at[k], b_s.at[p, k], b_r.at[p, k], axis[orders[p][1]])
        else:
            last(p, k, ra[p].at[k])

    def level_two(p, k):
        if len(orders[p]) > 1:
            landed(rb[p].at[k], b_s.at[p, k], b_r.at[p, k])
            kept = columns(p, ra[p].at[k], x) if orders[p][1] == "x" else ra[p].at[k, y]
            rb[p][k] = added(rb[p][k], kept[...])
            last(p, k, rb[p].at[k])

    def last(p, k, total):
        if k < NZ - 1:
            send(total, rz[p].at[k], z_s.at[p, k], z_r.at[p, k], device_at(x, goal(k), y, core))

    for step in range(NZ + 2):
        for level, work in enumerate((level_zero, level_one, level_two)):
            k = step - level
            if 0 <= k < NZ:
                for p in range(n):
                    work(p, k)
    for p in range(n):
        for k in range(NZ - 1):
            landed(rz[p].at[k], z_s.at[p, k], z_r.at[p, k])
        total = (rb if len(orders[p]) > 1 else ra)[p][NZ - 1].astype(jnp.float32)
        for k in range(NZ - 1):
            total = total + rz[p][k].astype(jnp.float32)
        out[p][...] = total
    for item in sent:
        item.wait_send()


def scatter_blocks(blocks, orders, use_x, collective_id):
    n = len(orders)
    dma = pltpu.SemaphoreType.DMA
    times = 2 if use_x else 1
    fulls = [b.shape[:-3] + b.shape[-2:] for b in blocks]
    outs = [f[:-1] + (f[-1] // times,) for f in fulls]

    def buffers(shapes):
        return [pltpu.VMEM(s, jnp.bfloat16) for s in shapes]

    whole = pl.BlockSpec(memory_space=pltpu.VMEM)
    return pl.pallas_call(
        functools.partial(scatter_kernel, orders, use_x),
        out_shape=[jax.ShapeDtypeStruct(o, jnp.float32) for o in outs],
        in_specs=[whole] * n,
        out_specs=[whole] * n,
        scratch_shapes=buffers([(NZ, NY) + f for f in fulls])
        + buffers([(NZ, NY) + o if r[0] == "x" else (NZ,) + f for r, f, o in zip(orders, fulls, outs)])
        + buffers([((NZ if len(r) > 1 else 1),) + o for r, o in zip(orders, outs)])
        + buffers([(NZ - 1,) + o for o in outs])
        + [dma((n, NZ, NY))] * 2
        + [dma((n, NZ))] * 4
        + [dma((n, NZ - 1))] * 2,
        compiler_params=pltpu.CompilerParams(
            collective_id=collective_id, has_side_effects=True, vmem_limit_bytes=48 * 1024 * 1024
        ),
    )(*blocks)


PAIR = 2 * HEAD_DIM
SCALE = 1.0 / math.sqrt(HEAD_DIM)


def head_rows(rows):
    first = lax.broadcasted_iota(jnp.int32, rows.shape, 1) < HEAD_DIM
    zero = jnp.zeros_like(rows)
    return jnp.concatenate([jnp.where(first, rows, zero), jnp.where(first, zero, rows)])


def head_columns(both):
    block = both.shape[0] // 2
    first = lax.broadcasted_iota(jnp.int32, (block, PAIR), 1) < HEAD_DIM
    return jnp.where(first, both[:block], both[block:])


def along(one, two, dims):
    return lax.dot_general(one, two, ((dims[0], dims[1]), ((), ())), preferred_element_type=jnp.float32)


def pair_probs(length, query, keys):
    scores = along(query, keys, ((1,), (1,))) * SCALE
    at = lax.broadcasted_iota(jnp.int32, scores.shape, 1)
    masked = jnp.where(at < length, scores, MASK_FILL)
    peak = jnp.max(masked, axis=-1, keepdims=True)
    log_total = peak + jnp.log(jnp.sum(jnp.exp(masked - peak), axis=-1, keepdims=True))
    return jnp.exp(masked - log_total)


def pair_of(kv_ref):
    size = kv_ref.shape[0] * kv_ref.shape[3]
    return kv_ref[:, 0, 0].reshape(size, PAIR), kv_ref[:, 1, 0].reshape(size, PAIR)


def attend_kernel(len_ref, q_ref, kv_ref, out_ref):
    keys, values = pair_of(kv_ref)
    probs = pair_probs(len_ref[pl.program_id(0)], head_rows(q_ref[...]), keys)
    both = along(probs.astype(jnp.bfloat16), values, ((1,), (0,)))
    out_ref[...] = head_columns(both).astype(jnp.bfloat16)


def attend_back_kernel(len_ref, q_ref, kv_ref, grad_ref, dq_ref, dkv_ref):
    keys, values = pair_of(kv_ref)
    query, grad = head_rows(q_ref[...]), head_rows(grad_ref[...])
    probs = pair_probs(len_ref[pl.program_id(0)], query, keys)
    grad_probs = along(grad, values, ((1,), (1,)))
    inner = jnp.sum(probs * grad_probs, axis=-1, keepdims=True)
    grad_scores = (probs * (grad_probs - inner)).astype(jnp.bfloat16)
    dq_ref[...] = (head_columns(along(grad_scores, keys, ((1,), (0,)))) * SCALE).astype(jnp.bfloat16)
    shape = dkv_ref.shape[0], dkv_ref.shape[3], PAIR
    dkv_ref[:, 0, 0] = (along(grad_scores, query, ((0,), (0,))) * SCALE).reshape(shape).astype(dkv_ref.dtype)
    dkv_ref[:, 1, 0] = along(probs.astype(jnp.bfloat16), grad, ((0,), (0,))).reshape(shape).astype(dkv_ref.dtype)


def attend_call(lengths, query, kv, grad, low):
    count, block = kv.shape[2:4]
    rows = pl.BlockSpec((block, PAIR), lambda s, h: (s, h))
    kv_spec = pl.BlockSpec((kv.shape[0], 2, 1, block, PAIR), lambda s, h: (0, 0, s, 0, h))
    small = pl.BlockSpec(memory_space=pltpu.SMEM)
    rows_out = jax.ShapeDtypeStruct(query.shape, jnp.bfloat16)
    grid = (count, HEADS // 2)
    params = pltpu.CompilerParams(vmem_limit_bytes=48 * 1024 * 1024)
    if grad is None:
        return pl.pallas_call(
            attend_kernel,
            grid=grid,
            out_shape=rows_out,
            in_specs=[small, rows, kv_spec],
            out_specs=rows,
            compiler_params=params,
        )(lengths, query, kv)
    return pl.pallas_call(
        attend_back_kernel,
        grid=grid,
        out_shape=[rows_out, jax.ShapeDtypeStruct(kv.shape, low)],
        in_specs=[small, rows, kv_spec, rows],
        out_specs=[rows, kv_spec],
        compiler_params=params,
    )(lengths, query, kv, grad)


ORDERS = (("x", "y"), ("y", "x"), ("y", "x"), ("x", "y"), ("y", "x"))
ORDERS_BACK = tuple(order[::-1] for order in ORDERS)


def split_three(values):
    high = values.astype(jnp.bfloat16)
    rest = values - high.astype(jnp.float32)
    middle = rest.astype(jnp.bfloat16)
    lowest = (rest - middle.astype(jnp.float32)).astype(jnp.bfloat16)
    return jnp.stack([high, middle, lowest])


def in_rows(values, lead, rows, width):
    flat = values.reshape(lead + (-1,))
    pad = [(0, 0)] * len(lead) + [(0, rows * width - flat.shape[-1])]
    return jnp.pad(flat, pad).reshape(lead + (rows, width))


def on_device(
    tokens,
    lengths,
    cotangent,
    attend_weight,
    attend_first,
    attend_second,
    output_weight,
    output_first,
    output_second,
    expand_weight,
    expand_first,
    expand_second,
    contract_weight,
    contract_first,
    contract_second,
    vector_params,
    vector_first,
    vector_second,
):
    block, count, width = tokens.shape
    token_rows = block * count
    n_fsdp, n_ctx = lax.axis_size("fsdp"), lax.axis_size("ctx")
    own_topology = (n_fsdp, n_ctx) == (2, NZ * NY * NCORE)
    low = jnp.bfloat16 if own_topology else jnp.float32
    depth, wide = attend_weight.shape[1:]
    nvec = vector_params.shape[0]
    vec_rows = -(-3 * nvec // (depth * 32)) * 32
    owns = [
        attend_weight.astype(jnp.bfloat16).transpose(0, 2, 1),
        output_weight.astype(jnp.bfloat16).T,
        expand_weight.astype(jnp.bfloat16).T,
        contract_weight.astype(jnp.bfloat16).T,
        in_rows(split_three(vector_params), (), vec_rows, depth),
    ]
    if own_topology:
        fulls = gather_blocks(owns, ORDERS, True, 1)
    else:
        fulls = []
        for own in owns:
            wider = lax.all_gather(own, "fsdp", axis=own.ndim - 1, tiled=True)
            fulls.append(lax.all_gather(wider, "ctx", axis=own.ndim - 2))
    attend_back = fulls[0].reshape(3, D, D)
    output_back = fulls[1].reshape(D, D)
    expand_back = fulls[2].reshape(FF, D)
    contract_back = fulls[3].reshape(D, FF)
    thirds = fulls[4][:, :, :depth].reshape(n_ctx, -1)[:, : 3 * nvec].reshape(n_ctx, 3, nvec)
    thirds = lax.optimization_barrier(thirds).astype(jnp.float32)
    vector = ((thirds[:, 0] + thirds[:, 1]) + thirds[:, 2]).reshape(-1)
    bias_query = vector[0:D]
    bias_value = vector[D : 2 * D]
    bias_out = vector[2 * D : 3 * D]
    bias_contract = vector[3 * D : 4 * D]
    gain_one = vector[4 * D : 5 * D]
    shift_one = vector[5 * D : 6 * D]
    gain_two = vector[6 * D : 7 * D]
    shift_two = vector[7 * D : 8 * D]
    bias_expand = vector[8 * D : 8 * D + FF]
    rows_in = tokens.transpose(1, 0, 2).reshape(token_rows, width)
    proj = jnp.einsum("td,ced->cte", rows_in, attend_back, preferred_element_type=jnp.float32)
    query = (proj[0] + bias_query).astype(jnp.bfloat16)
    keys_values = jnp.stack([proj[1], proj[2] + bias_value]).astype(jnp.bfloat16).reshape(2 * token_rows, width)
    if own_topology:
        (kv,) = gather_blocks([keys_values], (("y",),), False, 2)
    else:
        kv = lax.all_gather(keys_values, "ctx")
    kv = kv.reshape(n_ctx, 2, count, block, width)
    context = attend_call(lengths, query, kv, None, low)
    attn = jnp.einsum("te,de->td", context, output_back, preferred_element_type=jnp.float32) + bias_out
    mixed, normed_one, inverse_one = norm_parts(
        rows_in.astype(jnp.float32) + attn, gain_one, shift_one
    )
    mixed_low = mixed.astype(jnp.bfloat16)
    pre = jnp.einsum("td,fd->tf", mixed_low, expand_back, preferred_element_type=jnp.float32) + bias_expand
    act, gelu_back = jax.vjp(exact_gelu, pre)
    act_low = act.astype(jnp.bfloat16)
    ffn = jnp.einsum("tf,df->td", act_low, contract_back, preferred_element_type=jnp.float32) + bias_contract
    layer_out, normed_two, inverse_two = norm_parts(mixed + ffn, gain_two, shift_two)
    grad_out = cotangent.transpose(1, 0, 2).reshape(token_rows, width).astype(jnp.float32)
    grad_gain_two = jnp.sum(grad_out * normed_two, axis=0)
    grad_shift_two = jnp.sum(grad_out, axis=0)
    grad_resid = norm_back(grad_out, normed_two, inverse_two, gain_two)
    grad_ffn = grad_resid.astype(jnp.bfloat16)
    grad_bias_contract = jnp.sum(grad_ffn, axis=0, dtype=jnp.float32)
    grad_contract = jnp.einsum("tf,td->df", act_low, grad_ffn, preferred_element_type=jnp.float32)
    grad_act = jnp.einsum("td,df->tf", grad_ffn, contract_back, preferred_element_type=jnp.float32)
    grad_pre = gelu_back(grad_act)[0].astype(jnp.bfloat16)
    grad_bias_expand = jnp.sum(grad_pre, axis=0, dtype=jnp.float32)
    grad_expand = jnp.einsum("td,tf->fd", mixed_low, grad_pre, preferred_element_type=jnp.float32)
    grad_mixed = grad_resid + jnp.einsum(
        "tf,fd->td", grad_pre, expand_back, preferred_element_type=jnp.float32
    )
    grad_gain_one = jnp.sum(grad_mixed * normed_one, axis=0)
    grad_shift_one = jnp.sum(grad_mixed, axis=0)
    grad_attn = norm_back(grad_mixed, normed_one, inverse_one, gain_one)
    grad_attn_low = grad_attn.astype(jnp.bfloat16)
    grad_bias_out = jnp.sum(grad_attn_low, axis=0, dtype=jnp.float32)
    grad_output = jnp.einsum(
        "te,td->de", context, grad_attn_low, preferred_element_type=jnp.float32
    )
    grad_context = jnp.einsum(
        "td,de->te", grad_attn_low, output_back, preferred_element_type=jnp.float32
    ).astype(jnp.bfloat16)
    grad_query, grad_kv = attend_call(lengths, query, kv, grad_context, low)
    grad_kv = grad_kv.reshape(n_ctx, 2 * token_rows, width)
    if own_topology:
        (summed,) = scatter_blocks([grad_kv], (("y",),), False, 3)
    else:
        summed = lax.psum_scatter(grad_kv, "ctx", scatter_dimension=0)
    grad_keys_low, grad_values_low = summed.astype(jnp.bfloat16).reshape(2, token_rows, width)
    stacked = jnp.stack([grad_query, grad_keys_low, grad_values_low])
    grad_attend = jnp.einsum("td,cte->ced", rows_in, stacked, preferred_element_type=jnp.float32)
    tokens_grad = grad_attn + jnp.einsum(
        "cte,ced->td", stacked, attend_back, preferred_element_type=jnp.float32
    )
    grad_vector = jnp.concatenate(
        [
            jnp.sum(grad_query, axis=0, dtype=jnp.float32),
            jnp.sum(grad_values_low, axis=0, dtype=jnp.float32),
            grad_bias_out,
            grad_bias_contract,
            grad_gain_one,
            grad_shift_one,
            grad_gain_two,
            grad_shift_two,
            grad_bias_expand,
        ]
    )
    vector_blocks = in_rows(grad_vector.reshape(n_ctx, nvec), (n_ctx,), vec_rows, depth)
    blocks = [
        grad_attend.astype(low).reshape(3, n_ctx, wide, D),
        grad_output.astype(low).reshape(n_ctx, wide, D),
        grad_expand.astype(low).reshape(n_ctx, FF // n_ctx, D),
        grad_contract.astype(low).reshape(n_ctx, wide, FF),
        jnp.concatenate([vector_blocks.astype(low)] * n_fsdp, axis=2),
    ]
    if own_topology:
        owned = scatter_blocks(blocks, ORDERS_BACK, True, 4)
    else:
        owned = []
        for item in blocks:
            part = lax.psum_scatter(item, "ctx", scatter_dimension=item.ndim - 3)
            owned.append(lax.psum_scatter(part, "fsdp", scatter_dimension=part.ndim - 1, tiled=True))
    vector_owned = owned[4].reshape(-1)[:nvec]
    owned = [jnp.swapaxes(item, -1, -2) for item in owned[:4]]
    attend_new = adam_step(
        attend_weight, attend_first, attend_second, owned[0], RATE_ATTEND, WEIGHT_DECAY
    )
    output_new = adam_step(
        output_weight, output_first, output_second, owned[1], RATE_OUTPUT, WEIGHT_DECAY
    )
    expand_new = adam_step(
        expand_weight, expand_first, expand_second, owned[2], RATE_EXPAND, WEIGHT_DECAY
    )
    contract_new = adam_step(
        contract_weight, contract_first, contract_second, owned[3], RATE_CONTRACT, WEIGHT_DECAY
    )
    vector_new = adam_step(
        vector_params, vector_first, vector_second, vector_owned, RATE_VECTOR, 0.0
    )
    return (
        layer_out.astype(jnp.bfloat16).reshape(count, block, width).transpose(1, 0, 2),
        tokens_grad.reshape(count, block, width).transpose(1, 0, 2),
        attend_new[0],
        attend_new[1],
        attend_new[2],
        output_new[0],
        output_new[1],
        output_new[2],
        expand_new[0],
        expand_new[1],
        expand_new[2],
        contract_new[0],
        contract_new[1],
        contract_new[2],
        vector_new[0],
        vector_new[1],
        vector_new[2],
    )


def solution(mesh):
    in_specs = (
        P("ctx", "fsdp", None),
        P("fsdp"),
        P("ctx", "fsdp", None),
        P(None, "fsdp", "ctx"),
        P(None, "fsdp", "ctx"),
        P(None, "fsdp", "ctx"),
        P("fsdp", "ctx"),
        P("fsdp", "ctx"),
        P("fsdp", "ctx"),
        P("fsdp", "ctx"),
        P("fsdp", "ctx"),
        P("fsdp", "ctx"),
        P("fsdp", "ctx"),
        P("fsdp", "ctx"),
        P("fsdp", "ctx"),
        P("ctx"),
        P("ctx"),
        P("ctx"),
    )
    out_specs = (
        P("ctx", "fsdp", None),
        P("ctx", "fsdp", None),
        P(None, "fsdp", "ctx"),
        P(None, "fsdp", "ctx"),
        P(None, "fsdp", "ctx"),
        P("fsdp", "ctx"),
        P("fsdp", "ctx"),
        P("fsdp", "ctx"),
        P("fsdp", "ctx"),
        P("fsdp", "ctx"),
        P("fsdp", "ctx"),
        P("fsdp", "ctx"),
        P("fsdp", "ctx"),
        P("fsdp", "ctx"),
        P("ctx"),
        P("ctx"),
        P("ctx"),
    )
    return jax.shard_map(
        on_device, mesh=mesh, in_specs=in_specs, out_specs=out_specs, check_vma=False
    )
```

time: 1100 us -> 386 us (0.35)
  waiting for transfers between devices: 474 us -> 0 us
  blocking collectives: 424 us -> 0 us
  Pallas kernels: 0 us -> 325 us
  local copies, waits for them, and re-layouts: 74.2 us -> 7.85 us
  matrix products: 68.9 us -> 33.3 us
  other arithmetic: 34.6 us -> 18 us
  between operations: 16.6 us -> 1.3 us
    unnamed x3 -> x0, blocking collectives: 396 us -> none
    pallas_call x0 -> x6, Pallas kernels: none -> 325 us  [the longest x2 150 us: scatter_blocks(): pl.pallas_call(functools.partial(scatter_kernel, orders, use_x), out_shap...]
    reduce_scatter x8 -> x0, waiting for transfers between devices: 295 us -> none  [the longest x1 115 us: on_device(): lax.psum_scatter(grad_expand, 'ctx', scatter_dimension=1, tiled=True)]
    all_gather x6 -> x0, waiting for transfers between devices: 178 us -> none  [the longest x1 52.4 us: on_device(): lax.all_gather(row_tiles[2], 'ctx', axis=1, tiled=True)]
    dot_general x18 -> x12, matrix products: 68.9 us -> 33.3 us  [the longest x1 6.73 us: on_device(): jnp.einsum('td,fd->tf', mixed_low, expand_back, preferred_element_type=jn...]
    reshape x7, local copies, waits for them, and re-layouts: 29.2 us -> 2.86 us  [the longest x1 1.05 us: on_device(): tokens_grad.reshape(count, block, width).transpose(1, 0, 2)]
    all_gather x4 -> x0, blocking collectives: 23.3 us -> none  [the longest x1 6.75 us: on_device(): lax.all_gather(attend_weight.astype(jnp.bfloat16), 'fsdp', axis=1, tiled=...]
    all_gather x2 -> x0, local copies, waits for them, and re-layouts: 15.7 us -> none  [the longest x1 8.67 us: on_device(): lax.all_gather(local_keys, 'ctx', axis=0, tiled=True)]
  transfers between devices with their start and end apart: 14 -> 0, of which waited for: 8 -> 0; matrix products, arithmetic and copies ran while one was open for 8% -> 0% of each run, Pallas kernels for 0% -> 0%
where the time goes in v2:
time: 386 us; the launch traced here: 385 us
  Pallas kernels  325 us (84%)
  matrix products  33.3 us (9%)
  other arithmetic  18 us (5%)
  local copies, waits for them, and re-layouts  7.85 us (2%)
    pallas_call x2, Pallas kernels, scatter_blocks(): pl.pallas_call(functools.partial(scatter_kernel, orders, use_x), out_shap...  150 us
    pallas_call x2, Pallas kernels, gather_blocks(): pl.pallas_call(functools.partial(gather_kernel, orders, use_x), out_shape...  148 us
    pallas_call x1, Pallas kernels, attend_call(): pl.pallas_call(attend_back_kernel, grid=grid, out_shape=[rows_out, jax.Sh...  14.7 us
    pallas_call x1, Pallas kernels, attend_call(): pl.pallas_call(attend_kernel, grid=grid, out_shape=rows_out, in_specs=[sm...  11.7 us

profile of v2, /device:TPU:0, one launch (start us, length us, event | category | flops | bytes accessed | tf_op | source)
XLA Modules:
  0.0 385.5 jit_solution(4555270482689550689)
XLA Ops:
  0.7 0.8 fusion.49
  1.5 0.1 reshape.176
  1.6 0.6 reshape.177.refs_4_
  2.2 1.6 convert_bitcast_fusion.1.refs_3_
  3.8 1.6 convert_bitcast_fusion.2.refs_2_
  5.5 1.6 convert_bitcast_fusion.3.refs_0_
  7.1 1.5 convert_bitcast_fusion.4.refs_1_
  8.6 79.7 %shard_map.305 = (bf16[3,16,48,768]{3,2,1,0:T(8,128)(2,1)}, bf16[16,48,768]{2,1,0:T(8,128)(2,1)}, bf16[16,192,768]{2,1,0:T(8,128)(2,1)}, bf16[16,48,3072]{2,1,0:T(8,128)(2,1)}, bf16[16,32,768]{2,1,0:T(8,128)(2,1)}) custom-call(bf16[3,48,384]{2,1,0:T(8,128)(2,1)} %convert_bitcast_fusion.3.refs_0_, bf16[48,384]{1,0:T(8,128)(2,1)} %convert_bitcast_fusion.4.refs_1_, ...), custom_call_target="tpu_custom_call" | custom-call | tf_op jit(solution)/shard_map/pallas_call | solution.py:191
  88.4 1.0 slice.58
  89.4 0.1 copy.52
  89.6 0.1 reshape.180
  89.7 0.2 fusion.23
  89.9 0.1 add.178
  89.9 0.6 fusion.48
  90.6 3.3 convolution_bitcast_fusion
  93.9 0.8 pad_maximum_fusion.2
  94.7 68.3 %shard_map.306 = bf16[16,256,768]{2,1,0:T(8,128)(2,1)} custom-call(bf16[256,768]{1,0:T(8,128)(2,1)} %bitcast.136), custom_call_target="tpu_custom_call" | custom-call | tf_op jit(solution)/shard_map/pallas_call | solution.py:191
  163.1 11.7 %shard_map.307 = bf16[128,768]{1,0:T(8,128)(2,1)S(1)} custom-call(s32[2]{0:T(128)S(1)} %copy-done, bf16[128,768]{1,0:T(8,128)(2,1)S(1)} %fusion.12.q_ref, bf16[16,2,2,64,768]{4,3,2,1,0:T(8,128)(2,1)} %bitcast.113), custom_call_target="tpu_custom_call" | custom-call | tf_op jit(solution)/shard_map/pallas_call | solution.py:386
  174.9 0.6 fusion.50
  175.5 0.2 multiply_reduce_fusion.4
  175.8 0.0 copy-start.24
  175.8 6.7 %multiply_convert_fusion = (bf16[128,3072]{1,0:T(8,128)(2,1)S(1)}, f32[128,3072]{1,0:T(8,128)}, f32[128,3072]{1,0:T(8,128)}) fusion(f32[3072]{0:T(1024)S(1)} %slice.87, bf16[3072,768]{1,0:T(8,128)(2,1)S(1)} %bitcast.123, f32[128,768]{1,0:T(8,128)S(1)} %get-tuple-element.86, f32[768]{0:T(1024)S(1)} %get-tuple-element.77, f32[768]{0:T(1024)S(1)} %get-tuple-element.78, ...), kind=kOutput, calls=%fused_computation.7 | convolution fusion | flops 630423552 | bytes 9063424 | tf_op jit(solution)/shard_map/td,fd->tf/dot_general | solution.py:495
  182.6 1.8 fusion.51
  184.4 0.0 copy-start.23
  184.4 0.2 multiply_reduce_fusion.3
  184.6 0.8 fusion.47
  185.5 1.5 fusion.13
  186.9 0.3 fusion.9
  187.2 0.1 copy.48
  187.3 0.1 div.109
  187.4 0.8 convert_reduce_fusion.1
  188.2 5.7 %fusion.52 = (bf16[3072]{0:T(1024)(128)(2,1)}, bf16[128,3072]{1,0:T(8,128)(2,1)S(1)}) fusion(f32[128,3072]{1,0:T(8,128)} %get-tuple-element.67, f32[128,3072]{1,0:T(8,128)} %get-tuple-element.87, bf16[768,3072]{1,0:T(8,128)(2,1)} %bitcast.127, f32[128,768]{1,0:T(8,128)S(1)} %get-tuple-element.63), kind=kOutput, calls=%fused_computation.122 | convolution fusion | flops 609973248 | bytes 9050112 | tf_op jit(solution)/shard_map/td,df->tf/dot_general | solution.py:507
  193.9 1.5 multiply_reduce_fusion
  195.4 0.8 convert_reduce_fusion
  196.2 0.3 convolution_convert_fusion.4.grad_ref
  196.5 14.7 %shard_map.308 = (bf16[128,768]{1,0:T(8,128)(2,1)S(1)}, bf16[16,2,2,64,768]{4,3,2,1,0:T(8,128)(2,1)}) custom-call(s32[2]{0:T(128)S(1)} %copy-done, bf16[128,768]{1,0:T(8,128)(2,1)S(1)} %fusion.12.q_ref, bf16[16,2,2,64,768]{4,3,2,1,0:T(8,128)(2,1)} %bitcast.114, bf16[128,768]{1,0:T(8,128)(2,1)S(1)} %convolution_convert_fusion.4.grad_ref), custom_call_target="tpu_custom_call" | custom-call | tf_op jit(solution)/shard_map/pallas_call | solution.py:394
  211.2 67.6 %shard_map.309 = f32[256,768]{1,0:T(8,128)S(1)} custom-call(bf16[16,256,768]{2,1,0:T(8,128)(2,1)} %bitcast.118), custom_call_target="tpu_custom_call" | custom-call | tf_op jit(solution)/shard_map/pallas_call | solution.py:305
  278.9 0.8 slice_reduce_fusion
  279.7 0.2 dynamic-update-slice
  280.0 0.2 dynamic-update-slice.1
  280.2 0.2 dynamic-update-slice.2
  280.4 0.2 dynamic-update-slice.3
  280.6 0.2 dynamic-update-slice.4
  280.8 0.2 dynamic-update-slice.5
  281.0 0.4 dynamic-update-slice.6
  281.4 0.2 dynamic-update-slice.7
  281.7 0.1 reshape.192
  281.9 0.1 pad_maximum_fusion.refs_4_
  282.0 3.6 convolution_convert_fusion
  285.6 3.6 convolution_convert_fusion.1
  289.2 0.5 convolution_convert_fusion.3
  289.7 0.4 copy-done.9
  290.1 0.1 copy-done.10
  290.2 3.0 convolution_convert_fusion.2
  293.2 82.9 %shard_map.310 = (f32[3,48,384]{2,1,0:T(8,128)S(1)}, f32[48,384]{1,0:T(8,128)S(1)}, f32[192,384]{1,0:T(8,128)S(1)}, f32[48,1536]{1,0:T(8,128)S(1)}, f32[32,384]{1,0:T(8,128)S(1)}) custom-call(bf16[3,16,48,768]{3,2,1,0:T(8,128)(2,1)} %bitcast.117, bf16[16,48,768]{2,1,0:T(8,128)(2,1)S(1)} %bitcast.110, bf16[16,192,768]{2,1,0:T(8,128)(2,1)} %bitcast.115, ...), custom_call_target="tpu_custom_call" | custom-call | tf_op jit(solution)/shard_map/pallas_call | solution.py:305
  376.2 1.0 multiply_subtract_fusion
  377.3 0.1 copy-done.17
  377.4 1.0 multiply_subtract_fusion.1
  378.5 0.9 multiply_subtract_fusion.2
  379.5 0.7 multiply_subtract_fusion.3
  380.2 0.6 multiply_subtract_fusion.4
  380.8 2.7 fusion.8
  383.5 1.1 copy.56
  384.6 0.9 copy.57
  (117 shorter events, 0.6 us)
Async XLA Ops:
  5.5 85.1 %copy-start.20 = (bf16[64,2,768]{2,1,0:T(2,128)(2,1)S(1)}, bf16[64,2,768]{2,1,0:T(2,128)(2,1)}, u32[]{:S(2)}) copy-start(bf16[64,2,768]{2,1,0:T(2,128)(2,1)} %param.18) | copy-start | bytes 589828
  94.7 68.4 %copy-start = (s32[2]{0:T(128)S(1)}, s32[2]{0:T(128)}, u32[]{:S(2)}) copy-start(s32[2]{0:T(128)} %len_ref.3) | copy-start | bytes 28
  163.1 12.7 %slice-start = ((s8[4718592]{0:T(1024)(128)(4,1)}), s8[4194304]{0:T(1024)(128)(4,1)S(1)}, s32[]{:S(2)}) async-start(s8[4718592]{0:T(1024)(128)(4,1)} %bitcast.121), calls=%async_computation | async-start | bytes 8388608
  163.1 11.7 %copy-start.1 = (bf16[16,48,768]{2,1,0:T(8,128)(2,1)S(1)}, bf16[16,48,768]{2,1,0:T(8,128)(2,1)}, u32[]{:S(2)}) copy-start(bf16[16,48,768]{2,1,0:T(8,128)(2,1)} %get-tuple-element.31) | copy-start | bytes 3538948
  163.1 12.6 %slice-start.1 = ((s8[4718592]{0:T(1024)(128)(4,1)}), s8[524288]{0:T(1024)(128)(4,1)S(1)}, s32[]{:S(2)}) async-start(s8[4718592]{0:T(1024)(128)(4,1)} %bitcast.121), calls=%async_computation.1 | async-start | bytes 1048576
  174.9 7.7 %slice-start.4 = ((s8[4718592]{0:T(1024)(128)(4,1)}), s8[4194304]{0:T(1024)(128)(4,1)S(1)}, s32[]{:S(2)}) async-start(s8[4718592]{0:T(1024)(128)(4,1)} %bitcast.128), calls=%async_computation.4 | async-start | bytes 8388608
  175.5 7.0 %copy-start.26 = (f32[128]{0:T(128)}, f32[128]{0:T(128)S(1)}, u32[]{:S(2)}) copy-start(f32[128]{0:T(128)S(1)} %broadcast_multiply_fusion.4) | copy-start | bytes 1540
  175.7 6.8 %copy-start.28 = (f32[128]{0:T(128)}, f32[128]{0:T(128)S(1)}, u32[]{:S(2)}) copy-start(f32[128]{0:T(128)S(1)} %add_rsqrt_fusion.1) | copy-start | bytes 1540
  175.8 6.8 %slice-start.5 = ((s8[4718592]{0:T(1024)(128)(4,1)}), s8[524288]{0:T(1024)(128)(4,1)S(1)}, s32[]{:S(2)}) async-start(s8[4718592]{0:T(1024)(128)(4,1)} %bitcast.128), calls=%async_computation.5 | async-start | bytes 1048576
  175.8 6.8 %copy-start.24 = (f32[768]{0:T(1024)S(1)}, f32[768]{0:T(1024)}, u32[]{:S(2)}) copy-start(f32[768]{0:T(1024)} %get-tuple-element.76) | copy-start | bytes 9220
  182.5 1.8 copy-start.4
  182.6 2.0 copy-start.11
  184.4 1.1 copy-start.23
  187.4 6.5 %slice-start.2 = ((s8[4718592]{0:T(1024)(128)(4,1)}), s8[4194304]{0:T(1024)(128)(4,1)S(1)}, s32[]{:S(2)}) async-start(s8[4718592]{0:T(1024)(128)(4,1)} %bitcast.124), calls=%async_computation.2 | async-start | bytes 8388608
  188.2 5.7 %slice-start.3 = ((s8[4718592]{0:T(1024)(128)(4,1)}), s8[524288]{0:T(1024)(128)(4,1)S(1)}, s32[]{:S(2)}) async-start(s8[4718592]{0:T(1024)(128)(4,1)} %bitcast.124), calls=%async_computation.3 | async-start | bytes 1048576
  188.2 5.7 %copy-start.27 = (f32[128]{0:T(128)S(1)}, f32[128]{0:T(128)}, u32[]{:S(2)}) copy-start(f32[128]{0:T(128)} %copy-done.26) | copy-start | bytes 1540
  188.2 5.7 %copy-start.29 = (f32[128]{0:T(128)S(1)}, f32[128]{0:T(128)}, u32[]{:S(2)}) copy-start(f32[128]{0:T(128)} %copy-done.28) | copy-start | bytes 1540
  196.2 15.0 %copy-start.2 = (f32[128,768]{1,0:T(8,128)}, f32[128,768]{1,0:T(8,128)S(1)}, u32[]{:S(2)}) copy-start(f32[128,768]{1,0:T(8,128)S(1)} %get-tuple-element.65) | copy-start | bytes 1179652
  278.8 1.4 copy-start.36
  278.8 1.6 copy-start.33
  278.8 1.8 copy-start.35
  278.8 2.0 copy-start.34
  278.8 2.2 copy-start.32
  278.8 2.6 copy-start.31
  278.8 2.8 copy-start.37
  278.9 3.1 copy-start.5
  282.0 3.6 copy-start.30
  285.6 3.6 copy-start.3
  289.2 0.9 copy-start.9
  289.2 1.0 copy-start.10
  293.2 83.0 %copy-start.6 = (f32[1536,48]{0,1:T(8,128)S(1)}, f32[1536,48]{0,1:T(8,128)}, u32[]{:S(2)}) copy-start(f32[1536,48]{0,1:T(8,128)} %param.30) | copy-start | bytes 884740
  293.2 83.0 %copy-start.14 = (f32[1536,48]{0,1:T(8,128)S(1)}, f32[1536,48]{0,1:T(8,128)}, u32[]{:S(2)}) copy-start(f32[1536,48]{0,1:T(8,128)} %param.31) | copy-start | bytes 884740
  293.2 83.0 %copy-start.15 = (f32[1536,48]{0,1:T(8,128)S(1)}, f32[1536,48]{0,1:T(8,128)}, u32[]{:S(2)}) copy-start(f32[1536,48]{0,1:T(8,128)} %param.32) | copy-start | bytes 884740
  376.1 1.1 copy-start.7
  376.1 1.1 copy-start.16
  376.2 1.3 copy-start.17
  376.2 2.3 copy-start.8
  376.2 2.3 copy-start.18
  376.2 2.3 copy-start.19
  377.4 2.0 copy-start.13
  377.4 2.0 copy-start.21
  377.4 2.0 copy-start.22
  378.5 1.7 copy-start.25
  378.5 1.7 copy-start.38
  378.5 1.7 copy-start.39
  380.8 3.8 copy-start.12
